TPU v7x, 32 devices: a whole 2x2x4 slice. The times are simulated.
32 devices in a mesh: edge: 16 (over z, y, x), rep: 2 (over core).
Axes of the slice: x: 2, y: 2, z: 4, core: 2. Of those that a mesh axis runs over, the one named last changes fastest.
Arguments:
- node_feat: float32 [2, 8192, 14], P('rep', 'edge'), may hold values from -6 to 6
- node_types: int32 [2, 8192], P('rep', 'edge'), may hold values from 0 to 8
- boundary: int32 [2, 8192], P('rep', 'edge'), may hold values from 0 to 1
- target: float32 [2, 8192, 2], P('rep', 'edge'), may hold values from -6 to 6
- edge_feat: float32 [2, 131072, 3], P('rep', 'edge'), may hold values from -6 to 6
- senders: int32 [2, 131072], P('rep', 'edge'), may hold values from 0 to 8191, as said below
- receivers: int32 [2, 131072], P('rep', 'edge'), may hold values from 0 to 8191, as said below
- edge_counts: int32 [2, 16], P('rep', 'edge'), may hold values from 4096 to 8192, as said below
- mats: float32 [24, 128, 128], replicated, may hold values from -0.5 to 0.5
- vecs: float32 [60, 128], replicated
- mats_momentum: float32 [24, 128, 128], replicated, may hold values from -0.25 to 0.25
- vecs_momentum: float32 [60, 128], replicated, may hold values from -0.25 to 0.25
- factors: float32 [24, 128, 8], replicated, may hold values from -6 to 6
- errors: float32 [2, 24, 128, 128], P('rep'), may hold values from -0.25 to 0.25
Outputs:
- loss_sum: float32 [], replicated
- loss_count: float32 [], replicated
- stats: float32 [4, 2], replicated
- new_mats: float32 [24, 128, 128], replicated
- new_mats_momentum: float32 [24, 128, 128], replicated
- new_factors: float32 [24, 128, 8], replicated
- new_errors: float32 [2, 24, 128, 128], P('rep')
- new_vecs: float32 [60, 128], replicated
- new_vecs_momentum: float32 [60, 128], replicated
Inputs may be any that keep to these rules, and one draw needn't show every extreme that they name: `edge_counts`: multiples of 128; the live slots of a device come first; in each scene some device has all 8192 slots live. `receivers`: every edge slot of device d of a scene has its receiver among the particles d * 512 to (d + 1) * 512 - 1. `senders`: each sender lies within 512 particles of its edge's receiver.
All inputs are finite; a program needn't handle non-finite values.
Results may differ from a plain program's by a relative error of at most 0.0003.
Values sent between devices are 32-bit elements; how exact they have to be, the bound alone decides.
A program may use at most 256 MiB of HBM per device.

v0:
```python
from functools import partial

import jax
import jax.numpy as jnp
from jax import lax
from jax.sharding import PartitionSpec as P

NFEAT = 14
NTYPES = 9
EFEAT = 3
STEPS = 2


HIGH = lax.Precision.HIGHEST


def extended(cells, sides, width):
    for axis, dim in sides:
        count = lax.axis_size(axis)
        ends = count - 1
        head = lax.slice_in_dim(cells, 0, width, axis=dim)
        tail = lax.slice_in_dim(cells, cells.shape[dim] - width, cells.shape[dim], axis=dim)
        cells = jnp.concatenate(
            [
                lax.ppermute(tail, axis, [(i, (i + 1) % count) for i in range(ends)]),
                cells,
                lax.ppermute(head, axis, [((i + 1) % count, i) for i in range(ends)]),
            ],
            axis=dim,
        )
    return cells


def product(a, b):
    return jnp.dot(a, b, precision=HIGH)


def block_rows():
    return 512


def pick_rows(table, index):
    count = index.shape[0]
    size = block_rows()
    columns = jnp.arange(table.shape[0], dtype=jnp.int32)

    def pick_one_block(block_index):
        onehot = (block_index[:, None] == columns[None, :]).astype(jnp.float32)
        return product(onehot, table)

    picked = lax.map(pick_one_block, index.reshape(count // size, size))
    return picked.reshape(count, table.shape[1])


def add_rows(values, index, total_rows):
    count = index.shape[0]
    size = block_rows()
    columns = jnp.arange(total_rows, dtype=jnp.int32)

    def add_one_block(total, pieces):
        block_index, block_values = pieces
        onehot = (block_index[:, None] == columns[None, :]).astype(jnp.float32)
        return (total + jnp.dot(onehot.T, block_values, precision=HIGH), None)

    start = jnp.zeros((total_rows, values.shape[1]), jnp.float32)
    total, unused = lax.scan(
        add_one_block,
        start,
        (index.reshape(count // size, size), values.reshape(count // size, size, values.shape[1])),
    )
    return total


def layer_norm(v, gain, offset):
    cent = v - jnp.mean(v, -1, keepdims=True)
    var = jnp.mean(cent * cent, -1, keepdims=True)
    return cent * lax.rsqrt(var + 1e-05) * gain + offset


def mlp_tail(first, mats, vecs, second, third, which):
    base = NFEAT + NTYPES + EFEAT + 5 * which
    hidden = jax.nn.silu(first + vecs[base])
    hidden = jax.nn.silu(product(hidden, mats[second]) + vecs[base + 1])
    hidden = product(hidden, mats[third]) + vecs[base + 2]
    return layer_norm(hidden, vecs[base + 3], vecs[base + 4])


def encode_nodes(feat, types, mats, vecs):
    onehot = (types[:, None] == jnp.arange(NTYPES)[None, :]).astype(jnp.float32)
    first = product(feat, vecs[:NFEAT]) + product(onehot, vecs[NFEAT : NFEAT + NTYPES])
    return mlp_tail(first, mats, vecs, 0, 1, 0)


def encode_edges(efeat, mats, vecs):
    lead = NFEAT + NTYPES
    return mlp_tail(product(efeat, vecs[lead : lead + EFEAT]), mats, vecs, 2, 3, 1)


def edge_update(step, mats, vecs, edge, sent, recvd):
    base = 6 + 9 * step
    first = (
        product(edge, mats[base]) + product(sent, mats[base + 1]) + product(recvd, mats[base + 2])
    )
    return mlp_tail(first, mats, vecs, base + 3, base + 4, 2 + 2 * step)


def node_update(step, mats, vecs, node, agg):
    base = 6 + 9 * step
    first = product(node, mats[base + 5]) + product(agg, mats[base + 6])
    return mlp_tail(first, mats, vecs, base + 7, base + 8, 3 + 2 * step)


def decode(mats, vecs, node):
    base = NFEAT + NTYPES + EFEAT + 5 * (2 + 2 * STEPS)
    hidden = jax.nn.silu(product(node, mats[4]) + vecs[base])
    hidden = jax.nn.silu(product(hidden, mats[5]) + vecs[base + 1])
    return product(hidden, vecs[base + 2 : base + 4].T)


def orthonormal(left):
    columns = []
    for col in range(left.shape[-1]):
        vector = left[:, :, col]
        for prior in columns:
            vector = vector - jnp.sum(prior * vector, 1, keepdims=True) * prior
        vector = vector * lax.rsqrt(jnp.sum(vector * vector, 1, keepdims=True) + 1e-12)
        columns.append(vector)
    return jnp.stack(columns, -1)


def shards(
    node_feat,
    node_types,
    boundary,
    target,
    edge_feat,
    senders,
    receivers,
    edge_counts,
    mats,
    vecs,
    mats_momentum,
    vecs_momentum,
    factors,
    errors,
):
    feat = node_feat[0]
    goal = target[0]
    keep = (1 - boundary[0]).astype(jnp.float32)[:, None]
    own = feat.shape[0]
    place = lax.axis_index("edge")
    recv_local = receivers[0] - place * own
    send_at = senders[0] - (place - 1) * own
    wide_rows = 3 * own
    live = (jnp.arange(send_at.shape[0]) < edge_counts[0, 0]).astype(jnp.float32)[:, None]
    node, node_enc_back = jax.vjp(partial(encode_nodes, feat, node_types[0]), mats, vecs)
    edge, edge_enc_back = jax.vjp(partial(encode_edges, edge_feat[0]), mats, vecs)
    saved = []
    for step in range(STEPS):
        wide = extended(node, (("edge", 0),), own)
        sent = pick_rows(wide, send_at)
        recvd = pick_rows(node, recv_local)
        raw, edge_back = jax.vjp(partial(edge_update, step), mats, vecs, edge, sent, recvd)
        message = raw * live
        agg = add_rows(message, recv_local, own)
        delta, node_back = jax.vjp(partial(node_update, step), mats, vecs, node, agg)
        saved.append((edge_back, node_back))
        node = node + delta
        edge = edge + message
    pred, dec_back = jax.vjp(decode, mats, vecs, node)
    diff = pred - goal
    velocity = feat[:, 8:10]
    terms = jnp.stack(
        [
            jnp.sum(velocity * keep, 0),
            jnp.sum(velocity * velocity * keep, 0),
            jnp.sum(goal * keep, 0),
            jnp.sum(goal * goal * keep, 0),
        ]
    )
    count, loss_total, stat_sums = lax.psum(
        (jnp.sum(keep), jnp.sum(diff * diff * keep), terms), ("edge", "rep")
    )
    grad_m, grad_v, d_node = dec_back(2.0 * diff * keep / count)
    d_edge = jnp.zeros_like(edge)
    for step in reversed(range(STEPS)):
        edge_back, node_back = saved[step]
        part_m, part_v, d_self, d_agg = node_back(d_node)
        grad_m = grad_m + part_m
        grad_v = grad_v + part_v
        d_node = d_node + d_self
        d_message = (pick_rows(d_agg, recv_local) + d_edge) * live
        part_m, part_v, d_from_edge, d_sent, d_recvd = edge_back(d_message)
        grad_m = grad_m + part_m
        grad_v = grad_v + part_v
        d_edge = d_edge + d_from_edge
        d_node = d_node + add_rows(d_recvd, recv_local, own)
        spread = add_rows(d_sent, send_at, wide_rows)
        rims = jnp.stack([spread[:own], spread[2 * own :]])
        got = extended(rims, (("edge", 0),), 1)
        d_node = d_node + spread[own : 2 * own] + got[0] + got[3]
    part_m, part_v = node_enc_back(d_node)
    grad_m = grad_m + part_m
    grad_v = grad_v + part_v
    part_m, part_v = edge_enc_back(d_edge)
    grad_m, grad_v = lax.psum((grad_m + part_m, grad_v + part_v), "edge")
    with_error = grad_m + errors[0]
    left_part = jnp.einsum("kij,kjr->kir", with_error, factors, precision=HIGH)
    left, vec_grad = lax.psum((left_part, grad_v), "rep")
    left = orthonormal(left)
    right_part = jnp.einsum("kij,kir->kjr", with_error, left, precision=HIGH)
    right = lax.psum(right_part, "rep")
    approx = jnp.einsum("kir,kjr->kij", left, right, precision=HIGH)
    mats_mom = 0.9 * mats_momentum + approx
    vecs_mom = 0.9 * vecs_momentum + vec_grad
    return (
        loss_total,
        count,
        stat_sums / count,
        mats - 4.0 * mats_mom,
        mats_mom,
        right,
        (with_error - approx)[None],
        vecs - 4.0 * vecs_mom,
        vecs_mom,
    )


def solution(mesh):
    placed = (
        P("rep", "edge", None),
        P("rep", "edge"),
        P("rep", "edge"),
        P("rep", "edge", None),
        P("rep", "edge", None),
        P("rep", "edge"),
        P("rep", "edge"),
        P("rep", "edge"),
        P(),
        P(),
        P(),
        P(),
        P(),
        P("rep", None, None, None),
    )
    return jax.shard_map(
        shards,
        mesh=mesh,
        in_specs=placed,
        out_specs=(P(), P(), P(), P(), P(), P(), P("rep", None, None, None), P(), P()),
        check_vma=False,
    )
```

profile of v0, /device:TPU:0, one launch (start us, length us, event | category | flops | bytes accessed | tf_op | source)
XLA Modules:
  0.0 1260.2 jit_solution(489987520134507503)
XLA Ops:
  16.5 6.2 collective-permute-start
  30.1 37.2 %while.133 = (s32[]{:T(128)}, f32[16,512,128]{2,1,0:T(8,128)}, s32[16,512]{1,0:T(8,128)S(1)}, f32[512,128]{1,0:T(8,128)}, s32[]{:T(128)}) while((s32[]{:T(128)}, f32[16,512,128]{2,1,0:T(8,128)}, s32[16,512]{1,0:T(8,128)S(1)}, f32[512,128]{1,0:T(8,128)}, s32[]{:T(128)}) %tuple.357), condition=%wide.region_7.8_spmd.clone, body=%wide.region_6.7_spmd.clone.sunk | while | flops 402915328 | bytes 530509 | solution.py:51
  67.4 7.4 convolution_add_fusion.15
  79.1 5.8 fusion.419
  86.6 8.5 fusion.108
  102.0 55.2 %while.132 = (s32[]{:T(128)}, f32[16,512,128]{2,1,0:T(8,128)}, s32[16,512]{1,0:T(8,128)S(1)}, f32[1536,128]{1,0:T(8,128)}, s32[]{:T(128)}) while((s32[]{:T(128)}, f32[16,512,128]{2,1,0:T(8,128)}, s32[16,512]{1,0:T(8,128)S(1)}, f32[1536,128]{1,0:T(8,128)}, s32[]{:T(128)}) %tuple.354), condition=%wide.region_5.6_spmd.clone, body=%wide.region_4.5_spmd.clone.sunk | while | flops 1208745984 | bytes 1054797 | solution.py:51
  157.2 6.4 convolution_add_fusion.12
  171.6 5.4 fusion.420
  181.8 5.6 copy.78
  187.4 34.0 %while.138 = (s32[]{:T(128)}, f32[512,128]{1,0:T(8,128)S(1)}, s32[16,512]{1,0:T(8,128)S(1)}, f32[16,512,128]{2,1,0:T(8,128)}, s32[]{:T(128)}, /*index=5*/s32[]{:T(128)}) while((s32[]{:T(128)}, f32[512,128]{1,0:T(8,128)S(1)}, s32[16,512]{1,0:T(8,128)S(1)}, f32[16,512,128]{2,1,0:T(8,128)}, s32[]{:T(128)}, ...), condition=%wide.region_11.12_spmd.clone, body=%wide.region_10.11_spmd.clone.sunk | while | flops 403046400 | bytes 792671 | solution.py:66
  225.5 5.5 collective-permute-start.2
  233.5 36.8 %while.135 = (s32[]{:T(128)}, f32[16,512,128]{2,1,0:T(8,128)}, s32[16,512]{1,0:T(8,128)S(1)}, f32[512,128]{1,0:T(8,128)}, s32[]{:T(128)}) while((s32[]{:T(128)}, f32[16,512,128]{2,1,0:T(8,128)}, s32[16,512]{1,0:T(8,128)S(1)}, f32[512,128]{1,0:T(8,128)}, s32[]{:T(128)}) %tuple.401), condition=%wide.region_17.18_spmd.clone, body=%wide.region_16.17_spmd.clone.sunk | while | flops 402915328 | bytes 530509 | solution.py:51
  270.3 10.7 fusion.247
  286.7 55.1 %while.134 = (s32[]{:T(128)}, f32[16,512,128]{2,1,0:T(8,128)}, s32[16,512]{1,0:T(8,128)S(1)}, f32[1536,128]{1,0:T(8,128)}, s32[]{:T(128)}) while((s32[]{:T(128)}, f32[16,512,128]{2,1,0:T(8,128)}, s32[16,512]{1,0:T(8,128)S(1)}, f32[1536,128]{1,0:T(8,128)}, s32[]{:T(128)}) %tuple.407), condition=%wide.region_15.16_spmd.clone, body=%wide.region_14.15_spmd.clone.sunk | while | flops 1208745984 | bytes 1054797 | solution.py:51
  341.8 6.4 convolution_add_fusion.8
  356.2 5.4 fusion.422
  366.3 5.6 copy.79
  372.0 34.0 %while.139 = (s32[]{:T(128)}, f32[512,128]{1,0:T(8,128)S(1)}, s32[16,512]{1,0:T(8,128)S(1)}, f32[16,512,128]{2,1,0:T(8,128)}, s32[]{:T(128)}, /*index=5*/s32[]{:T(128)}) while((s32[]{:T(128)}, f32[512,128]{1,0:T(8,128)S(1)}, s32[16,512]{1,0:T(8,128)S(1)}, f32[16,512,128]{2,1,0:T(8,128)}, s32[]{:T(128)}, ...), condition=%wide.region_21.22_spmd.clone, body=%wide.region_20.21_spmd.clone.sunk | while | flops 403046400 | bytes 792671 | solution.py:66
  412.0 43.3 %all-reduce.60 = (f32[]{:T(128)}, f32[]{:T(128)}, f32[4,2]{1,0:T(4,128)S(1)}) all-reduce(f32[]{:T(128)} %get-tuple-element.591, f32[]{:T(128)} %fusion.408, f32[4,2]{1,0:T(4,128)S(1)} %pad_maximum_fusion.2), channel_id=1, replica_groups=mesh['edge'=16,'rep'=2] {'edge','rep'}, use_global_device_ids=true, to_apply=%region_25.26 | all-reduce | flops 10 | bytes 80 | tf_op jit(solution)/shard_map/psum | solution.py:181
  479.7 21.6 %while.136 = (s32[]{:T(128)}, f32[16,512,128]{2,1,0:T(8,128)}, s32[16,512]{1,0:T(8,128)S(1)}, f32[512,128]{1,0:T(8,128)S(1)}, s32[]{:T(128)}) while((s32[]{:T(128)}, f32[16,512,128]{2,1,0:T(8,128)}, s32[16,512]{1,0:T(8,128)S(1)}, f32[512,128]{1,0:T(8,128)S(1)}, s32[]{:T(128)}) %tuple.403), condition=%wide.region_36.37_spmd.clone, body=%wide.region_35.36_spmd.clone.sunk | while | flops 402915328 | bytes 530509 | solution.py:51
  501.3 5.8 copy.80
  507.1 5.9 multiply_reduce_fusion.2
  515.2 8.0 fusion.133
  523.2 8.6 fusion.433
  531.9 8.5 convolution_bitcast_fusion.11
  540.4 5.1 fusion.432
  545.5 5.6 convolution_bitcast_fusion.8
  551.1 7.7 convolution_bitcast_fusion.9
  558.8 7.8 convolution_bitcast_fusion.10
  566.6 5.0 fusion.214
  571.6 4.9 fusion.216
  581.2 88.4 %while.141 = (s32[]{:T(128)}, f32[1536,128]{1,0:T(8,128)}, s32[16,512]{1,0:T(8,128)}, f32[16,512,128]{2,1,0:T(8,128)}, s32[]{:T(128)}, /*index=5*/s32[]{:T(128)}) while((s32[]{:T(128)}, f32[1536,128]{1,0:T(8,128)}, s32[16,512]{1,0:T(8,128)}, f32[16,512,128]{2,1,0:T(8,128)}, s32[]{:T(128)}, /*index=5*/s32[]{:T(128)}) %tuple.408), condition=%wide.region_42.43_spmd.clone, body=%wide.region_41.42_spmd.clone.sunk | while | flops 1209139200 | bytes 1841247 | solution.py:66
  587.2 4.8 fusion.539
  598.3 4.8 fusion.539
  626.0 4.8 fusion.539
  653.7 4.8 fusion.539
  677.1 34.0 %while.140 = (s32[]{:T(128)}, f32[512,128]{1,0:T(8,128)S(1)}, s32[16,512]{1,0:T(8,128)S(1)}, f32[16,512,128]{2,1,0:T(8,128)}, s32[]{:T(128)}, /*index=5*/s32[]{:T(128)}) while((s32[]{:T(128)}, f32[512,128]{1,0:T(8,128)S(1)}, s32[16,512]{1,0:T(8,128)S(1)}, f32[16,512,128]{2,1,0:T(8,128)}, s32[]{:T(128)}, ...), condition=%wide.region_40.41_spmd.clone, body=%wide.region_39.40_spmd.clone.sunk | while | flops 403046400 | bytes 792671 | solution.py:66
  725.7 21.6 %while.137 = (s32[]{:T(128)}, f32[16,512,128]{2,1,0:T(8,128)}, s32[16,512]{1,0:T(8,128)S(1)}, f32[512,128]{1,0:T(8,128)S(1)}, s32[]{:T(128)}) while((s32[]{:T(128)}, f32[16,512,128]{2,1,0:T(8,128)}, s32[16,512]{1,0:T(8,128)S(1)}, f32[512,128]{1,0:T(8,128)S(1)}, s32[]{:T(128)}) %tuple.405), condition=%wide.region_46.47_spmd.clone, body=%wide.region_45.46_spmd.clone.sunk | while | flops 402915328 | bytes 530509 | solution.py:51
  747.4 5.8 copy.81
  753.2 11.0 multiply_reduce_fusion.1
  766.5 8.2 fusion.136
  774.8 8.1 fusion.429
  782.9 8.4 convolution_bitcast_fusion.7
  791.4 5.3 fusion.428
  796.6 7.6 convolution_bitcast_fusion.5
  804.2 7.4 convolution_bitcast_fusion.6
  811.6 5.6 fusion.132
  817.3 6.2 multiply_reduce_fusion
  825.8 8.4 fusion.139
  834.3 8.5 fusion.425
  842.8 8.0 convolution_bitcast_fusion.4
  850.8 6.7 fusion.424
  857.5 4.9 fusion.210
  862.4 4.9 fusion.212
  867.4 33.9 %while.142 = (s32[]{:T(128)}, f32[512,128]{1,0:T(8,128)S(1)}, s32[16,512]{1,0:T(8,128)S(1)}, f32[16,512,128]{2,1,0:T(8,128)}, s32[]{:T(128)}, /*index=5*/s32[]{:T(128)}) while((s32[]{:T(128)}, f32[512,128]{1,0:T(8,128)S(1)}, s32[16,512]{1,0:T(8,128)S(1)}, f32[16,512,128]{2,1,0:T(8,128)}, s32[]{:T(128)}, ...), condition=%wide.region_50.51_spmd.clone, body=%wide.region_49.50_spmd.clone.sunk | while | flops 403046400 | bytes 792671 | solution.py:66
  901.4 88.5 %while.143 = (s32[]{:T(128)}, f32[1536,128]{1,0:T(8,128)}, s32[16,512]{1,0:T(8,128)}, f32[16,512,128]{2,1,0:T(8,128)}, s32[]{:T(128)}, /*index=5*/s32[]{:T(128)}) while((s32[]{:T(128)}, f32[1536,128]{1,0:T(8,128)}, s32[16,512]{1,0:T(8,128)}, f32[16,512,128]{2,1,0:T(8,128)}, s32[]{:T(128)}, /*index=5*/s32[]{:T(128)}) %tuple.409), condition=%wide.region_52.53_spmd.clone, body=%wide.region_51.52_spmd.clone.sunk | while | flops 1209139200 | bytes 1841247 | solution.py:66
  929.6 4.8 fusion.542
  957.3 4.8 fusion.542
  985.0 4.8 fusion.542
  999.9 5.2 collective-permute-done.6
  1022.5 108.7 %all-reduce.65.cloned.1.call-done = f32[24,128,128]{2,1,0:T(8,128)} async-done(((f32[24,128,128]{2,1,0:T(8,128)}), f32[24,128,128]{2,1,0:T(8,128)}) %all-reduce.65.cloned.1.call-update) | async-done | bytes 1572880 | tf_op jit(solution)/shard_map/psum | solution.py:206
  1136.9 75.2 %psum.62 = f32[60,128]{1,0:T(8,128)S(1)} all-reduce(f32[60,128]{1,0:T(8,128)S(1)} %add_add_fusion.9), channel_id=1, replica_groups=mesh['edge'=16,'rep'=2] {'edge'}, use_global_device_ids=true, to_apply=%region_128.129 | all-reduce | flops 7680 | bytes 61440 | tf_op jit(solution)/shard_map/psum | solution.py:206
  1232.6 13.4 %all-reduce.69.cloned.1.call-done = f32[24,128,8]{1,2,0:T(8,128)} async-done(((f32[24,128,8]{1,2,0:T(8,128)}), f32[24,128,8]{1,2,0:T(8,128)}) %all-reduce.69.cloned.1.call-update) | async-done | bytes 98320 | tf_op jit(solution)/shard_map/psum | solution.py:212
  1246.1 6.8 multiply_subtract_fusion
  (879 shorter events, 687.6 us)
Async XLA Ops:
  7.2 1124.0 %copy-start = (f32[24,128,8]{1,2,0:T(8,128)S(1)}, f32[24,128,8]{1,2,0:T(8,128)}, u32[]{:S(2)}) copy-start(f32[24,128,8]{1,2,0:T(8,128)} %param.50) | copy-start | bytes 294916
  7.2 1124.0 %all-reduce.65.cloned.1.call-start = ((), (), s32[]{:S(2)}) async-start(), calls=%async_computation | async-start | bytes 3145728 | tf_op jit(solution)/shard_map/psum | solution.py:206
  8.8 77.8 %copy-start.88 = (f32[128]{0:T(128)}, f32[128]{0:T(128)S(1)}, u32[]{:S(2)}) copy-start(f32[128]{0:T(128)S(1)} %get-tuple-element.762) | copy-start | bytes 1540
  14.0 209.2 %copy-start.26 = (f32[512,128]{1,0:T(8,128)}, f32[512,128]{1,0:T(8,128)S(1)}, u32[]{:S(2)}) copy-start(f32[512,128]{1,0:T(8,128)S(1)} %get-tuple-element.773) | copy-start | bytes 786436
  14.0 53.4 %copy-start.38 = (f32[1,8192,3]{1,0,2:T(1,128)S(1)}, f32[1,8192,3]{1,0,2:T(1,128)}, u32[]{:S(2)}) copy-start(f32[1,8192,3]{1,0,2:T(1,128)} %param.42) | copy-start | bytes 294916
  14.0 209.1 %copy-start.69 = (f32[512]{0:T(512)}, f32[512]{0:T(512)S(1)}, u32[]{:S(2)}) copy-start(f32[512]{0:T(512)S(1)} %broadcast_multiply_fusion.8) | copy-start | bytes 6148
  14.3 60.5 %copy-start.91 = (f32[512]{0:T(512)}, f32[512]{0:T(512)S(1)}, u32[]{:S(2)}) copy-start(f32[512]{0:T(512)S(1)} %multiply_reduce_fusion.18) | copy-start | bytes 6148
  14.3 208.9 %copy-start.81 = (f32[512]{0:T(512)}, f32[512]{0:T(512)S(1)}, u32[]{:S(2)}) copy-start(f32[512]{0:T(512)S(1)} %fusion.375) | copy-start | bytes 6148
  15.2 82.4 %collective-permute-start.1 = (f32[512,128]{1,0:T(8,128)}, f32[512,128]{1,0:T(8,128)S(1)}, u32[]{:S(2)}, u32[]{:S(2)}) collective-permute-start(f32[512,128]{1,0:T(8,128)} %multiply_add_fusion.6), channel_id=1, source_target_pairs={{2,0},{4,2},{6,4},{8,6},{10,8},{12,10},{14,12},{16,14},{18,16},{20... | collective-permute-start | bytes 786440 | tf_op jit(solution)/shard_map/ppermute | solution.py:27
  16.5 81.1 %collective-permute-start = (f32[512,128]{1,0:T(8,128)}, f32[512,128]{1,0:T(8,128)}, u32[]{:S(2)}, u32[]{:S(2)}) collective-permute-start(f32[512,128]{1,0:T(8,128)} %multiply_add_fusion.6), channel_id=1, source_target_pairs={{0,2},{2,4},{4,6},{6,8},{8,10},{10,12},{12,14},{14,16},{16,18},{18... | collective-permute-start | bytes 786440 | tf_op jit(solution)/shard_map/ppermute | solution.py:25
  25.7 49.1 %copy-start.106 = (f32[1,512]{1,0:T(1,128)}, f32[1,512]{1,0:T(1,128)S(1)}, u32[]{:S(2)}) copy-start(f32[1,512]{1,0:T(1,128)S(1)} %subtract_convert_fusion) | copy-start | bytes 6148
  30.1 44.7 %copy-start.28 = (f32[24,128,128]{2,1,0:T(8,128)S(1)}, f32[24,128,128]{2,1,0:T(8,128)}, u32[]{:S(2)}) copy-start(f32[24,128,128]{2,1,0:T(8,128)} %param.46) | copy-start | bytes 4718596
  181.8 39.6 %copy-start.129 = (f32[128]{0:T(128)S(1)}, f32[128]{0:T(128)}, u32[]{:S(2)}) copy-start(f32[128]{0:T(128)} %get-tuple-element.756) | copy-start | bytes 1540
  187.4 34.8 %copy-start.138 = (f32[128]{0:T(128)S(1)}, f32[128]{0:T(128)}, u32[]{:S(2)}) copy-start(f32[128]{0:T(128)} %get-tuple-element.754) | copy-start | bytes 1540
  187.4 35.8 %copy-start.97 = (f32[128]{0:T(128)S(1)}, f32[128]{0:T(128)}, u32[]{:S(2)}) copy-start(f32[128]{0:T(128)} %copy-done.96) | copy-start | bytes 1540
  187.4 35.8 %copy-start.108 = (f32[128]{0:T(128)S(1)}, f32[128]{0:T(128)}, u32[]{:S(2)}) copy-start(f32[128]{0:T(128)} %get-tuple-element.753) | copy-start | bytes 1540
  187.4 35.8 %copy-start.112 = (f32[128]{0:T(128)S(1)}, f32[128]{0:T(128)}, u32[]{:S(2)}) copy-start(f32[128]{0:T(128)} %copy-done.111) | copy-start | bytes 1540
  187.4 35.8 %copy-start.128 = (f32[128]{0:T(128)S(1)}, f32[128]{0:T(128)}, u32[]{:S(2)}) copy-start(f32[128]{0:T(128)} %get-tuple-element.752) | copy-start | bytes 1540
  222.7 47.6 %copy-start.89 = (f32[128]{0:T(128)S(1)}, f32[128]{0:T(128)}, u32[]{:S(2)}) copy-start(f32[128]{0:T(128)} %copy-done.88) | copy-start | bytes 1540
  223.1 57.9 %copy-start.93 = (f32[512]{0:T(512)}, f32[512]{0:T(512)S(1)}, u32[]{:S(2)}) copy-start(f32[512]{0:T(512)S(1)} %multiply_reduce_fusion.17) | copy-start | bytes 6148
  224.3 58.1 %collective-permute-start.3 = (f32[512,128]{1,0:T(8,128)}, f32[512,128]{1,0:T(8,128)S(1)}, u32[]{:S(2)}, u32[]{:S(2)}) collective-permute-start(f32[512,128]{1,0:T(8,128)} %add_add_fusion.8), channel_id=1, source_target_pairs={{2,0},{4,2},{6,4},{8,6},{10,8},{12,10},{14,12},{16,14},{18,16},{20... | collective-permute-start | bytes 786440 | tf_op jit(solution)/shard_map/ppermute | solution.py:27
  225.5 56.8 %collective-permute-start.2 = (f32[512,128]{1,0:T(8,128)}, f32[512,128]{1,0:T(8,128)}, u32[]{:S(2)}, u32[]{:S(2)}) collective-permute-start(f32[512,128]{1,0:T(8,128)} %add_add_fusion.8), channel_id=1, source_target_pairs={{0,2},{2,4},{4,6},{6,8},{8,10},{10,12},{12,14},{14,16},{16,18},{18... | collective-permute-start | bytes 786440 | tf_op jit(solution)/shard_map/ppermute | solution.py:25
  366.3 39.6 %copy-start.125 = (f32[128]{0:T(128)S(1)}, f32[128]{0:T(128)}, u32[]{:S(2)}) copy-start(f32[128]{0:T(128)} %get-tuple-element.746) | copy-start | bytes 1540
  371.9 34.4 %copy-start.135 = (f32[128]{0:T(128)S(1)}, f32[128]{0:T(128)}, u32[]{:S(2)}) copy-start(f32[128]{0:T(128)} %get-tuple-element.745) | copy-start | bytes 1540
  371.9 34.9 %copy-start.134 = (f32[128]{0:T(128)S(1)}, f32[128]{0:T(128)}, u32[]{:S(2)}) copy-start(f32[128]{0:T(128)} %get-tuple-element.744) | copy-start | bytes 1540
  371.9 35.6 %copy-start.95 = (f32[128]{0:T(128)S(1)}, f32[128]{0:T(128)}, u32[]{:S(2)}) copy-start(f32[128]{0:T(128)} %get-tuple-element.740) | copy-start | bytes 1540
  371.9 35.6 %copy-start.110 = (f32[128]{0:T(128)S(1)}, f32[128]{0:T(128)}, u32[]{:S(2)}) copy-start(f32[128]{0:T(128)} %get-tuple-element.743) | copy-start | bytes 1540
  371.9 35.6 %copy-start.124 = (f32[128]{0:T(128)S(1)}, f32[128]{0:T(128)}, u32[]{:S(2)}) copy-start(f32[128]{0:T(128)} %get-tuple-element.742) | copy-start | bytes 1540
  371.9 37.8 %copy-start.133 = (f32[128]{0:T(128)S(1)}, f32[128]{0:T(128)}, u32[]{:S(2)}) copy-start(f32[128]{0:T(128)} %get-tuple-element.741) | copy-start | bytes 1540
  371.9 38.2 %copy-start.87 = (f32[1,512,14]{1,2,0:T(8,128)S(1)}, f32[1,512,14]{1,2,0:T(8,128)}, u32[]{:S(2)}) copy-start(f32[1,512,14]{1,2,0:T(8,128)} %copy.101) | copy-start | bytes 86020
  371.9 38.2 %copy-start.107 = (f32[1,512]{1,0:T(1,128)S(1)}, f32[1,512]{1,0:T(1,128)}, u32[]{:S(2)}) copy-start(f32[1,512]{1,0:T(1,128)} %copy-done.106) | copy-start | bytes 6148
  371.9 38.2 %copy-start.142 = (f32[1,512,2]{1,2,0:T(2,128)S(1)}, f32[1,512,2]{1,2,0:T(2,128)}, u32[]{:S(2)}) copy-start(f32[1,512,2]{1,2,0:T(2,128)} %param.41) | copy-start | bytes 12292
  405.9 49.4 %copy-start.132 = (f32[512]{0:T(512)S(1)}, f32[512]{0:T(512)}, u32[]{:S(2)}) copy-start(f32[512]{0:T(512)} %broadcast_multiply_fusion.5) | copy-start | bytes 6148
  406.3 54.3 %copy-start.53 = (f32[512,128]{1,0:T(8,128)}, f32[512,128]{1,0:T(8,128)S(1)}, u32[]{:S(2)}) copy-start(f32[512,128]{1,0:T(8,128)S(1)} %fusion.127) | copy-start | bytes 786436
  671.4 43.5 %copy-start.84 = (f32[512]{0:T(512)S(1)}, f32[512]{0:T(512)}, u32[]{:S(2)}) copy-start(f32[512]{0:T(512)} %copy-done.83) | copy-start | bytes 6148
  671.4 43.5 %copy-start.109 = (f32[128]{0:T(128)S(1)}, f32[128]{0:T(128)}, u32[]{:S(2)}) copy-start(f32[128]{0:T(128)} %get-tuple-element.753) | copy-start | bytes 1540
  671.4 42.8 %collective-permute-start.4 = (f32[1,512,128]{2,1,0:T(8,128)}, f32[1,512,128]{2,1,0:T(8,128)S(1)}, u32[]{:S(2)}, u32[]{:S(2)}) collective-permute-start(f32[1,512,128]{2,1,0:T(8,128)} %get-tuple-element.738), channel_id=1, source_target_pairs={{0,2},{2,4},{4,6},{6,8},{8,10},{10,12},{12,14},{14,16},{16,18},{18... | collective-permute-start | bytes 786440 | tf_op jit(solution)/shard_map/ppermute | solution.py:25
  675.8 38.4 %collective-permute-start.5 = (f32[1,512,128]{2,1,0:T(8,128)}, f32[1,512,128]{2,1,0:T(8,128)S(1)}, u32[]{:S(2)}, u32[]{:S(2)}) collective-permute-start(f32[1,512,128]{2,1,0:T(8,128)} %get-tuple-element.739), channel_id=1, source_target_pairs={{2,0},{4,2},{6,4},{8,6},{10,8},{12,10},{14,12},{16,14},{18,16},{20... | collective-permute-start | bytes 786440 | tf_op jit(solution)/shard_map/ppermute | solution.py:27
  901.3 96.0 %copy-start.24 = (f32[512,128]{1,0:T(8,128)S(1)}, f32[512,128]{1,0:T(8,128)}, u32[]{:S(2)}) copy-start(f32[512,128]{1,0:T(8,128)} %copy-done.23) | copy-start | bytes 786436
  901.3 96.6 %copy-start.37 = (f32[512,128]{1,0:T(8,128)S(1)}, f32[512,128]{1,0:T(8,128)}, u32[]{:S(2)}) copy-start(f32[512,128]{1,0:T(8,128)} %copy-done.36) | copy-start | bytes 786436
  901.3 96.6 %copy-start.104 = (f32[512]{0:T(512)S(1)}, f32[512]{0:T(512)}, u32[]{:S(2)}) copy-start(f32[512]{0:T(512)} %copy-done.103) | copy-start | bytes 6148
  901.3 105.6 %copy-start.27 = (f32[512,128]{1,0:T(8,128)S(1)}, f32[512,128]{1,0:T(8,128)}, u32[]{:S(2)}) copy-start(f32[512,128]{1,0:T(8,128)} %copy-done.26) | copy-start | bytes 786436
  901.3 105.6 %copy-start.70 = (f32[512]{0:T(512)S(1)}, f32[512]{0:T(512)}, u32[]{:S(2)}) copy-start(f32[512]{0:T(512)} %copy-done.69) | copy-start | bytes 6148
  901.4 105.6 %copy-start.82 = (f32[512]{0:T(512)S(1)}, f32[512]{0:T(512)}, u32[]{:S(2)}) copy-start(f32[512]{0:T(512)} %copy-done.81) | copy-start | bytes 6148
  901.4 105.6 %copy-start.98 = (f32[128]{0:T(128)S(1)}, f32[128]{0:T(128)}, u32[]{:S(2)}) copy-start(f32[128]{0:T(128)} %copy-done.96) | copy-start | bytes 1540
  991.0 14.1 %collective-permute-start.6 = (f32[1,512,128]{2,1,0:T(8,128)S(1)}, f32[1,512,128]{2,1,0:T(8,128)S(1)}, u32[]{:S(2)}, u32[]{:S(2)}) collective-permute-start(f32[1,512,128]{2,1,0:T(8,128)S(1)} %get-tuple-element.736), channel_id=1, source_target_pairs={{0,2},{2,4},{4,6},{6,8},{8,10},{10,12},{12,14},{14,16},{16,18},{18... | collective-permute-start | bytes 786440 | tf_op jit(solution)/shard_map/ppermute | solution.py:25
  995.6 11.4 collective-permute-start.7
  1013.2 202.5 %all-reduce.67.cloned.1.call-start = ((), (), s32[]{:S(2)}) async-start(), calls=%async_computation.1 | async-start | bytes 196608 | tf_op jit(solution)/shard_map/psum | solution.py:209
  1018.2 113.0 %copy-start.21 = (f32[1,24,128,128]{3,2,1,0:T(8,128)S(1)}, f32[1,24,128,128]{3,2,1,0:T(8,128)}, u32[]{:S(2)}) copy-start(f32[1,24,128,128]{3,2,1,0:T(8,128)} %param.51) | copy-start | bytes 4718596
  1018.2 117.8 %copy-start.113 = (f32[128]{0:T(128)S(1)}, f32[128]{0:T(128)}, u32[]{:S(2)}) copy-start(f32[128]{0:T(128)} %get-tuple-element.543) | copy-start | bytes 1540
  1018.2 117.8 %copy-start.114 = (f32[128]{0:T(128)S(1)}, f32[128]{0:T(128)}, u32[]{:S(2)}) copy-start(f32[128]{0:T(128)} %get-tuple-element.547) | copy-start | bytes 1540
  1018.2 117.8 %copy-start.115 = (f32[128]{0:T(128)S(1)}, f32[128]{0:T(128)}, u32[]{:S(2)}) copy-start(f32[128]{0:T(128)} %get-tuple-element.545) | copy-start | bytes 1540
  1018.2 117.8 %copy-start.116 = (f32[128]{0:T(128)S(1)}, f32[128]{0:T(128)}, u32[]{:S(2)}) copy-start(f32[128]{0:T(128)} %get-tuple-element.548) | copy-start | bytes 1540
  1018.2 117.8 %copy-start.117 = (f32[128]{0:T(128)S(1)}, f32[128]{0:T(128)}, u32[]{:S(2)}) copy-start(f32[128]{0:T(128)} %get-tuple-element.549) | copy-start | bytes 1540
  1018.2 117.8 %copy-start.118 = (f32[128]{0:T(128)S(1)}, f32[128]{0:T(128)}, u32[]{:S(2)}) copy-start(f32[128]{0:T(128)} %get-tuple-element.555) | copy-start | bytes 1540
  1018.3 117.8 %copy-start.119 = (f32[128]{0:T(128)S(1)}, f32[128]{0:T(128)}, u32[]{:S(2)}) copy-start(f32[128]{0:T(128)} %add_reduce_fusion.5) | copy-start | bytes 1540
  1018.3 117.8 %copy-start.120 = (f32[128]{0:T(128)S(1)}, f32[128]{0:T(128)}, u32[]{:S(2)}) copy-start(f32[128]{0:T(128)} %get-tuple-element.541) | copy-start | bytes 1540
  1018.3 117.8 %copy-start.121 = (f32[128]{0:T(128)S(1)}, f32[128]{0:T(128)}, u32[]{:S(2)}) copy-start(f32[128]{0:T(128)} %multiply_reduce_fusion.3) | copy-start | bytes 1540
  1018.3 117.8 %copy-start.122 = (f32[128]{0:T(128)S(1)}, f32[128]{0:T(128)}, u32[]{:S(2)}) copy-start(f32[128]{0:T(128)} %add_reduce_fusion.2) | copy-start | bytes 1540
  1021.3 114.8 %copy-start.123 = (f32[128]{0:T(128)S(1)}, f32[128]{0:T(128)}, u32[]{:S(2)}) copy-start(f32[128]{0:T(128)} %add_reduce_fusion.3) | copy-start | bytes 1540
  1022.5 209.5 %copy-start.65 = (f32[60,128]{1,0:T(8,128)S(1)}, f32[60,128]{1,0:T(8,128)}, u32[]{:S(2)}) copy-start(f32[60,128]{1,0:T(8,128)} %param.47) | copy-start | bytes 92164
  1022.5 209.5 %copy-start.85 = (f32[60,128]{1,0:T(8,128)S(1)}, f32[60,128]{1,0:T(8,128)}, u32[]{:S(2)}) copy-start(f32[60,128]{1,0:T(8,128)} %param.49) | copy-start | bytes 92164
  1131.2 98.7 %copy-start.22 = (f32[24,128,128]{2,1,0:T(8,128)S(1)}, f32[24,128,128]{2,1,0:T(8,128)}, u32[]{:S(2)}) copy-start(f32[24,128,128]{2,1,0:T(8,128)} %all-reduce.65.cloned.1.call-done) | copy-start | bytes 4718596
  1135.9 110.1 %all-reduce.69.cloned.1.call-start = ((), (), s32[]{:S(2)}) async-start(), calls=%async_computation.2 | async-start | bytes 196608 | tf_op jit(solution)/shard_map/psum | solution.py:212
  (105 other events, 864.2 us)
Sparse Core Ops, SparseCore 0:
  1013.3 117.7 all-reduce.64
  1136.0 17.1 all-reduce.66
  1232.1 13.9 all-reduce.68
where the time goes:
time: 1270 us; the launch traced here: 1260 us
  matrix products  826 us (65%)
  waiting for transfers between devices  129 us (10%)
  blocking collectives  122 us (10%)
  local copies, waits for them, and re-layouts  79.6 us (6%)
  other arithmetic  57.8 us (5%)
  starting transfers between devices  26.2 us (2%)
  between operations  16.9 us (1%)
    dot_general x177, matrix products, product(): return jnp.dot(a, b, precision=HIGH)  526 us
    dot_general x96, matrix products, add_one_block(): return (total + jnp.dot(onehot.T, block_values, precision=HIGH), None)  287 us
    psum x1, waiting for transfers between devices, shards(): grad_m, grad_v = lax.psum((grad_m + part_m, grad_v + part_v), 'edge')  109 us
    psum x1, blocking collectives, shards(): grad_m, grad_v = lax.psum((grad_m + part_m, grad_v + part_v), 'edge')  75.2 us
    psum x1, blocking collectives, shards(): lax.psum((jnp.sum(keep), jnp.sum(diff * diff * keep), terms), ('edge', 'r...  43.3 us
  transfers between devices with their start and end apart: 11, of which 4 were waited for; matrix products, arithmetic and copies ran while one was open for 14% of the time, Pallas kernels for 0%

commit v1 on v0

v1 whole, which is shorter than its diff:
```python
from functools import partial

import jax
import jax.numpy as jnp
from jax import lax
from jax.experimental import pallas as pl
from jax.experimental.pallas import tpu as pltpu
from jax.sharding import PartitionSpec as P

NFEAT = 14
NTYPES = 9
EFEAT = 3
LEAD = NFEAT + NTYPES
ROWS0 = LEAD + EFEAT
LAT = 128
BLOCK = 1024
F32 = jnp.float32
BF16 = jnp.bfloat16
NN = (((1,), (0,)), ((), ()))
NT = (((1,), (1,)), ((), ()))
TN = (((0,), (0,)), ((), ()))


def mm(a, b, dims=NN):
    return lax.dot_general(a, b, dims, preferred_element_type=F32)


def split(w):
    hi = w.astype(BF16)
    return hi, (w - hi.astype(F32)).astype(BF16)


def mm2(a, pair, dims=NN):
    return mm(a, pair[0], dims) + mm(a, pair[1], dims)


def mm3(a, b, dims=NN):
    ah, al = split(a)
    bh, bl = split(b)
    return mm(ah, bh, dims) + (mm(ah, bl, dims) + mm(al, bh, dims))


def silu_half(half):
    up = 1.0 + jnp.tanh(half)
    value = half * up
    sig = 0.5 * up
    return value, sig + value - value * sig


def rows_of(vecs_ref, which):
    base = ROWS0 + 5 * which
    return [vecs_ref[base + i : base + i + 1, :] for i in range(5)]


def mean_last(v):
    return jnp.mean(v, -1, keepdims=True)


def fold_rows(v):
    total = v[0:8]
    for i in range(8, v.shape[0], 8):
        total = total + v[i : i + 8]
    return total


def node_tail(first, second, third, vec):
    b1, b2, b3, g, o = vec
    s1, d1 = silu_half(0.5 * (first + b1))
    s2, d2 = silu_half(0.5 * (mm3(s1, second) + b2))
    z = mm3(s2, third) + b3
    c = z - mean_last(z)
    inv = lax.rsqrt(mean_last(c * c) + 1e-05)
    xhat = c * inv
    return xhat * g + o, (s1, d1, s2, d2, xhat, jnp.broadcast_to(inv, xhat.shape))


def node_tail_back(d, kept, second, third, vec):
    s1, d1, s2, d2, xhat, inv = kept
    g = vec[3]
    dy = d * g
    dz3 = inv * (dy - mean_last(dy) - xhat * mean_last(dy * xhat))
    dz2 = mm3(dz3, third, NT) * d2
    dz1 = mm3(dz2, second, NT) * d1
    sums = [fold_rows(v) for v in (dz1, dz2, dz3, d * xhat, d)]
    rows = [jnp.sum(v, 0, keepdims=True) for v in sums]
    return dz1, mm3(s1, dz2, TN), mm3(s2, dz3, TN), rows


def center(w):
    return w - mean_last(w)


def edge_tail(half, second, third, b2, b3, g, o, ones):
    s1, d1 = silu_half(half)
    s1 = s1.astype(BF16)
    s2, d2 = silu_half(mm2(s1, second) + b2)
    s2 = s2.astype(BF16)
    c = mm2(s2, third) + b3
    inv = lax.rsqrt(mm((c * c).astype(BF16), ones) + 1e-05)
    xhat = c * inv
    kept = (s1, d1, s2, d2, xhat.astype(BF16), inv)
    return xhat * g + o, kept


def edge_tail_back(d, kept, second, third, g, ones, grads, sums):
    s1, d1, s2, d2, xhat, inv = kept
    d1, d2, xhat, inv = (v[...].astype(F32) for v in (d1, d2, xhat, inv))
    dx = d * xhat
    dyx = (dx * g).astype(BF16)
    dc = inv * (d * g - xhat * mm(dyx, ones))
    dcb = dc.astype(BF16)
    dz2 = mm2(dcb, third, NT) * d2
    dz2b = dz2.astype(BF16)
    dz1 = mm2(dz2b, second, NT) * d1
    grads[0][...] += mm(s1[...], dz2b, TN)
    grads[1][...] += mm(s2[...], dcb, TN)
    for i, v in enumerate((dz1, dz2, dc, dx, d)):
        sums[i] += fold_rows(v)
    return dz1


def store_kept(refs, kept):
    for ref, v in zip(refs, kept):
        ref[...] = v


def put_pair(ref, at, w):
    hi, lo = split(w)
    ref[at] = hi
    ref[at + 1] = lo


def pair(ref, at):
    return ref[at], ref[at + 1]


def columns_of(code):
    parts = [
        jnp.transpose(jnp.broadcast_to(code[q : q + 1, :], (LAT, LAT))) for q in range(code.shape[0])
    ]
    return jnp.concatenate(parts, 0)


def pick_mask(column, count):
    lanes = lax.broadcasted_iota(jnp.int32, (column.shape[0], LAT), 1)
    parts = [
        jnp.where(column == lanes + LAT * j, 1.0, 0.0).astype(BF16) for j in range(count // LAT)
    ]
    return parts[0] if len(parts) == 1 else jnp.concatenate(parts, 1)


def add_mask(row, count):
    down = lax.broadcasted_iota(jnp.int32, (count, LAT), 0)
    parts = [
        jnp.where(row[q : q + 1, :] == down, 1.0, 0.0).astype(BF16) for q in range(row.shape[0])
    ]
    return jnp.concatenate(parts, 1)


def halves(v, upper):
    return jnp.concatenate([jnp.where(upper, 0.0, v), jnp.where(upper, v, 0.0)], 1)


def choose(wide, upper):
    return jnp.where(upper, wide[:, LAT:], wide[:, :LAT])


def send_of(code):
    return code >> 12


def recv_of(code):
    return code & 1023


def send_upper(code):
    return (code & 2048) != 0


def recv_upper(code):
    return (code & 1024) != 0


def fold_table(table):
    half = table.shape[0] // 2
    return jnp.concatenate([table[:half], table[half:]], 1)


def unfold(v):
    return jnp.concatenate([v[:, :LAT], v[:, LAT:]], 0)


def add_into(ref, code, column, values, recv_only=False):
    if not recv_only:
        ref[1][...] += mm(
            add_mask(send_of(code), ref[1].shape[0]),
            halves(values, send_upper(column)).astype(BF16),
        )
    mask = add_mask(recv_of(code), ref[0].shape[0])
    values = halves(values, recv_upper(column))
    if recv_only:
        ref[0][...] += mm2(mask, split(values))
    else:
        ref[0][...] += mm(mask, values.astype(BF16))


def encode_edges_kernel(x_ref, lo_ref, hi_ref, vecs_ref, e_ref, *rest):
    kept, w_ref = rest[:6], rest[6]
    b1, b2, b3, g, o = rows_of(vecs_ref, 1)

    @pl.when(pl.program_id(0) == 0)
    def _():
        put_pair(w_ref, 0, 0.5 * lo_ref[2])
        put_pair(w_ref, 2, center(hi_ref[0]))

    ones = jnp.full((LAT, LAT), 1.0 / LAT, BF16)
    xh, xl = split(x_ref[...])
    wh, wl = split(0.5 * vecs_ref[LEAD:ROWS0, :])
    half = mm(xh, wh) + (mm(xh, wl) + mm(xl, wh)) + 0.5 * b1
    out, saved = edge_tail(half, pair(w_ref, 0), pair(w_ref, 2), 0.5 * b2, center(b3), g, o, ones)
    e_ref[...] = out.astype(BF16)
    store_kept(kept, saved)


def edge_step(code_ref, e_ref, kept, w_ref, send_table, recv_table, vec, total):
    b1, b2, b3, g, o = vec
    ones = jnp.full((LAT, LAT), 1.0 / LAT, BF16)
    code = code_ref[...]
    column = columns_of(code)
    e = e_ref[...]
    half = mm2(e, pair(w_ref, 0)) + 0.5 * b1
    wide = mm2(pick_mask(send_of(column), send_table.shape[1]), pair(send_table, 0))
    half = half + choose(wide, send_upper(column))
    wide = mm2(pick_mask(recv_of(column), recv_table.shape[1]), pair(recv_table, 0))
    half = half + choose(wide, recv_upper(column))
    out, saved = edge_tail(half, pair(w_ref, 2), pair(w_ref, 4), 0.5 * b2, center(b3), g, o, ones)
    store_kept(kept, saved)
    add_into((total,), code, column, out, recv_only=True)
    return e, out


def put_edge_weights(w_ref, a, second, third):
    put_pair(w_ref, 0, 0.5 * a)
    put_pair(w_ref, 2, 0.5 * second)
    put_pair(w_ref, 4, center(third))


def forward_first_kernel(
    own, code_ref, e_ref, feat_ref, enc_ref, ma, mb, mc, na, vecs_ref, e_out, *rest
):
    kept, rest = rest[:6], rest[6:]
    wide_ref, enc_kept, agg_ref, upd_kept, h_ref, hb_ref, hc_ref = rest[:7]
    w_ref, send_table, recv_table, total = rest[7:]
    step = pl.program_id(0)

    @pl.when(step == 0)
    def _():
        put_edge_weights(w_ref, ma[0], mb[0], mb[1])
        types = lax.broadcasted_iota(jnp.int32, (NTYPES, feat_ref.shape[1]), 0).astype(F32)
        onehot = jnp.where(feat_ref[NFEAT : NFEAT + 1, :] == types, 1.0, 0.0)
        first = mm3(feat_ref[0:NFEAT, :], vecs_ref[0:NFEAT, :], TN)
        first = first + mm2(onehot.astype(BF16), split(vecs_ref[NFEAT:LEAD, :]), TN)
        out, saved = node_tail(first, enc_ref[0], enc_ref[1], rows_of(vecs_ref, 0))
        wide_ref[...] = out
        for i, v in enumerate(saved):
            enc_kept[i] = v
        put_pair(send_table, 0, fold_table(0.5 * mm3(out, ma[1])))
        put_pair(recv_table, 0, fold_table(0.5 * mm3(out[own : 2 * own], ma[2])))
        total[...] = jnp.zeros_like(total)

    e, out = edge_step(
        code_ref, e_ref, kept, w_ref, send_table, recv_table, rows_of(vecs_ref, 2), total
    )
    e_out[...] = (e.astype(F32) + out).astype(BF16)

    @pl.when(step == pl.num_programs(0) - 1)
    def _():
        h = wide_ref[own : 2 * own, :]
        agg = unfold(total[...])
        agg_ref[...] = agg
        first = mm3(h, mb[2]) + mm3(agg, mc[0])
        delta, saved = node_tail(first, mc[1], mc[2], rows_of(vecs_ref, 3))
        for i, v in enumerate(saved):
            upd_kept[i] = v
        h = h + delta
        h_ref[...] = h
        hb_ref[...] = 0.5 * mm3(h, na[1])
        hc_ref[...] = 0.5 * mm3(h, na[2])


def forward_second_kernel(
    own, code_ref, e_ref, left, mid, right, hc_ref, h_ref, ma, mb, mc, dec, vecs_ref, goal_ref,
    keep_ref, feat_ref, *rest
):
    kept, rest = rest[:6], rest[6:]
    dh_ref, dagg_ref, gm_ref, gv_ref, sums_ref = rest[:5]
    w_ref, send_table, recv_table, total = rest[5:]
    step = pl.program_id(0)

    @pl.when(step == 0)
    def _():
        put_edge_weights(w_ref, ma[0], mb[0], mb[1])
        table = jnp.concatenate([left[...], mid[...], right[...]], 0)
        put_pair(send_table, 0, fold_table(table))
        put_pair(recv_table, 0, fold_table(hc_ref[...]))
        total[...] = jnp.zeros_like(total)

    edge_step(code_ref, e_ref, kept, w_ref, send_table, recv_table, rows_of(vecs_ref, 4), total)

    @pl.when(step == pl.num_programs(0) - 1)
    def _():
        h = h_ref[...]
        agg = unfold(total[...])
        vec = rows_of(vecs_ref, 5)
        first = mm3(h, mb[2]) + mm3(agg, mc[0])
        delta, saved = node_tail(first, mc[1], mc[2], vec)
        out = h + delta
        base = ROWS0 + 30
        s1, d1 = silu_half(0.5 * (mm3(out, dec[1]) + vecs_ref[base : base + 1, :]))
        s2, d2 = silu_half(0.5 * (mm3(s1, dec[2]) + vecs_ref[base + 1 : base + 2, :]))
        last = vecs_ref[base + 2 : base + 4, :]
        keep = keep_ref[...]
        goal = goal_ref[...]
        diff = mm3(last, s2, NT) - goal
        kept_diff = diff * keep
        dpred = 2.0 * kept_diff
        dz2 = mm3(dpred, last, TN) * d2
        dz1 = mm3(dz2, dec[2], NT) * d1
        d = mm3(dz1, dec[1], NT)
        dz, g_second, g_third, rows = node_tail_back(d, saved, mc[1], mc[2], vec)
        dh_ref[...] = d + mm3(dz, mb[2], NT)
        dagg_ref[...] = mm3(dz, mc[0], NT)
        gm_ref[0] = mm3(out, dz1, TN)
        gm_ref[1] = mm3(s1, dz2, TN)
        gm_ref[2] = mm3(h, dz, TN)
        gm_ref[3] = mm3(agg, dz, TN)
        gm_ref[4] = g_second
        gm_ref[5] = g_third
        rows = rows + [
            jnp.sum(fold_rows(dz1), 0, keepdims=True),
            jnp.sum(fold_rows(dz2), 0, keepdims=True),
            mm3(dpred, s2),
        ]
        at = 0
        for v in rows:
            gv_ref[at : at + v.shape[0], :] = v
            at += v.shape[0]
        gv_ref[at:, :] = jnp.zeros((gv_ref.shape[0] - at, LAT), F32)
        velocity = feat_ref[8:10, :]
        pieces = [
            kept_diff * diff,
            velocity * keep,
            velocity * velocity * keep,
            goal * keep,
            goal * goal * keep,
            jnp.broadcast_to(keep, velocity.shape),
        ]
        for i, v in enumerate(pieces):
            part = v[:, 0:LAT]
            for j in range(LAT, own, LAT):
                part = part + v[:, j : j + LAT]
            sums_ref[2 * i : 2 * i + 2, :] = part
        sums_ref[12:16, :] = jnp.zeros((4, LAT), F32)


def backward_step(code_ref, kept, e_ref, dagg, de, w_ref, vec, gm, sums, totals):
    ones = jnp.full((LAT, LAT), 1.0 / LAT, BF16)
    code = code_ref[...]
    column = columns_of(code)
    wide = mm2(pick_mask(recv_of(column), dagg.shape[1]), pair(dagg, 0))
    d = choose(wide, recv_upper(column))
    if de is not None:
        d = d + de
    dz1 = edge_tail_back(
        d, kept, pair(w_ref, 2), pair(w_ref, 4), vec[3], ones, (gm.at[1], gm.at[2]), sums
    )
    dz1b = dz1.astype(BF16)
    gm[0] += mm(e_ref[...], dz1b, TN)
    add_into(totals, code, column, dz1)
    back = mm2(dz1b, pair(w_ref, 0), NT)
    return back if de is None else de + back


def finish_sums(sums):
    rows = [jnp.sum(sums[i], 0, keepdims=True) for i in range(5)]
    rows[2] = center(rows[2])
    return rows


def put_back_weights(w_ref, at, a, second, third):
    put_pair(w_ref, at, a)
    put_pair(w_ref, at + 2, second)
    put_pair(w_ref, at + 4, center(third))


def backward_second_kernel(own, code_ref, *rest):
    kept, rest = rest[:6], rest[6:]
    e_ref, dagg_ref, ma, mb, vecs_ref, de_out, gm, gv_ref, spread, s_recv = rest[:10]
    w_ref, dagg, sums, recv_total, send_total = rest[10:]
    step = pl.program_id(0)

    @pl.when(step == 0)
    def _():
        put_back_weights(w_ref, 0, ma[0], mb[0], mb[1])
        put_pair(dagg, 0, fold_table(dagg_ref[...]))
        gm[...] = jnp.zeros_like(gm)
        sums[...] = jnp.zeros_like(sums)
        recv_total[...] = jnp.zeros_like(recv_total)
        send_total[...] = jnp.zeros_like(send_total)

    de = backward_step(
        code_ref, kept, e_ref, dagg, None, w_ref, rows_of(vecs_ref, 4), gm, sums,
        (recv_total, send_total),
    )
    de_out[...] = de.astype(BF16)

    @pl.when(step == pl.num_programs(0) - 1)
    def _():
        gm[2] = center(gm[2])
        for i, v in enumerate(finish_sums(sums)):
            gv_ref[i : i + 1, :] = v
        gv_ref[5:8, :] = jnp.zeros((3, LAT), F32)
        spread[...] = unfold(send_total[...])
        s_recv[...] = unfold(recv_total[...])


def backward_first_kernel(own, code_ref, *rest):
    kept, rest = rest[:6], rest[6:]
    e_ref, rest = rest[0], rest[1:]
    enc_kept, rest = rest[:6], rest[6:]
    x_ref, de_ref, dh_ref, mid, from_left, from_right, s_recv, h_ref, rest = *rest[:8], rest[8:]
    wide_ref, node_kept, upd_kept, agg_ref, feat_ref, rest = *rest[:5], rest[5:]
    enc_lo, enc_hi, ma, mb, mc, na, vecs_ref, rest = *rest[:7], rest[7:]
    gm, gn, gv_ref = rest[:3]
    w_ref, dagg, sums, enc_sums, we_ref, dh0, recv_total, send_total = rest[3:]
    step = pl.program_id(0)

    @pl.when(step == 0)
    def _():
        put_back_weights(w_ref, 0, ma[0], mb[0], mb[1])
        put_pair(w_ref, 6, enc_lo[2])
        put_pair(w_ref, 8, center(enc_hi[0]))
        for ref in (gm, sums, enc_sums, we_ref, recv_total, send_total):
            ref[...] = jnp.zeros_like(ref)
        sent = mid[...] + from_left[...] + from_right[...]
        got = s_recv[...]
        h = h_ref[...]
        gn[0] = mm3(h, sent, TN)
        gn[1] = mm3(h, got, TN)
        d = dh_ref[...] + mm3(sent, na[1], NT) + mm3(got, na[2], NT)
        vec = rows_of(vecs_ref, 3)
        saved = [upd_kept[i] for i in range(6)]
        dz, g_second, g_third, rows = node_tail_back(d, saved, mc[1], mc[2], vec)
        gn[2] = mm3(wide_ref[own : 2 * own, :], dz, TN)
        gn[3] = mm3(agg_ref[...], dz, TN)
        gn[4] = g_second
        gn[5] = g_third
        for i, v in enumerate(rows):
            gv_ref[i : i + 1, :] = v
        dh0[...] = d + mm3(dz, mb[2], NT)
        put_pair(dagg, 0, fold_table(mm3(dz, mc[0], NT)))

    de = backward_step(
        code_ref, kept, e_ref, dagg, de_ref[...].astype(F32), w_ref, rows_of(vecs_ref, 2), gm, sums,
        (recv_total, send_total),
    )
    ones = jnp.full((LAT, LAT), 1.0 / LAT, BF16)
    dz1 = edge_tail_back(
        de, enc_kept, pair(w_ref, 6), pair(w_ref, 8), rows_of(vecs_ref, 1)[3], ones,
        (gm.at[3], gm.at[4]), enc_sums,
    )
    we_ref[...] += mm(x_ref[...].astype(BF16), dz1.astype(BF16), TN)

    @pl.when(step == pl.num_programs(0) - 1)
    def _():
        gm[2] = center(gm[2])
        gm[4] = center(gm[4])
        at = 5
        for v in finish_sums(sums) + finish_sums(enc_sums):
            gv_ref[at : at + 1, :] = v
            at += 1
        gv_ref[at : at + EFEAT, :] = we_ref[...]
        at += EFEAT
        sent = unfold(send_total[...])
        got = unfold(recv_total[...])
        h = wide_ref[...]
        gn[6] = mm3(h, sent, TN)
        gn[7] = mm3(h[own : 2 * own], got, TN)
        d = mm3(sent, ma[1], NT)
        inner = d[own : 2 * own] + dh0[...] + mm3(got, ma[2], NT)
        d = jnp.concatenate([d[:own], inner, d[2 * own :]], 0)
        saved = [node_kept[i] for i in range(6)]
        vec = rows_of(vecs_ref, 0)
        dz, g_second, g_third, rows = node_tail_back(d, saved, enc_lo[0], enc_lo[1], vec)
        gn[8] = g_second
        gn[9] = g_third
        types = lax.broadcasted_iota(jnp.int32, (NTYPES, feat_ref.shape[1]), 0).astype(F32)
        onehot = jnp.where(feat_ref[NFEAT : NFEAT + 1, :] == types, 1.0, 0.0)
        for v in rows:
            gv_ref[at : at + 1, :] = v
            at += 1
        gv_ref[at : at + NFEAT, :] = mm3(feat_ref[0:NFEAT, :], dz)
        at += NFEAT
        gv_ref[at : at + NTYPES, :] = mm2(onehot.astype(BF16), split(dz))
        at += NTYPES
        gv_ref[at:, :] = jnp.zeros((gv_ref.shape[0] - at, LAT), F32)


def whole(shape):
    return pl.BlockSpec(shape, lambda i: (0,) * len(shape))


def third(at):
    return pl.BlockSpec((3, LAT, LAT), lambda i: (at, 0, 0))


def edges(width):
    return pl.BlockSpec((BLOCK, width), lambda i: (i, 0))


CODE = pl.BlockSpec((BLOCK // LAT, LAT), lambda i: (i, 0))
KEPT = 6
KINDS = (BF16, F32, BF16, F32, BF16, F32)


def call(kernel, count, ins, outs, scratch):
    return pl.pallas_call(
        kernel,
        grid=(count // BLOCK,),
        in_specs=[spec for _, spec in ins],
        out_specs=[spec for _, _, spec in outs],
        out_shape=[jax.ShapeDtypeStruct(shape, kind) for shape, kind, _ in outs],
        scratch_shapes=scratch,
        compiler_params=pltpu.CompilerParams(
            dimension_semantics=("arbitrary",), vmem_limit_bytes=56 << 20
        ),
    )(*[array for array, _ in ins])


def full(shape):
    return (shape, F32, whole(shape))


def shifted(up, down):
    count = lax.axis_size("edge")
    ends = count - 1
    from_left = lax.ppermute(up, "edge", [(i, i + 1) for i in range(ends)])
    from_right = lax.ppermute(down, "edge", [(i + 1, i) for i in range(ends)])
    return from_left, from_right


SMALL = {"n1": 0, "e1": 16, "n0": 24, "sums": 72}
SMALL_ROWS = 88
PLACES = (
    (4, 5, 20, 21, 22, 23),
    (15, 18, 19),
    (6, 9, 10, 2, 3),
    (16, 17, 11, 12, 13, 14, 7, 8, 0, 1),
)


def sides_of(count):
    return {16: (2, 2, 4), 64: (4, 4, 4)}.get(count, (count, 1, 1))


class Reducer:
    def __init__(self, count, rows):
        sides = sides_of(count)
        strides = (1, sides[0], sides[0] * sides[1])
        dims = list(zip(sides, strides))
        self.orders = (dims, [dims[1], dims[0], dims[2]])
        self.rows = rows
        self.count = count
        self.copies = 2 * sum(k - 1 for k in sides)

    def scratch(self):
        shapes = []
        for order in self.orders:
            length = self.rows // 2
            for k, _ in order:
                length //= k
                shapes.append(pltpu.VMEM((max(k - 1, 1), length, LAT), F32))
        sems = [pltpu.SemaphoreType.DMA((2 * self.copies,))] * 2
        return shapes + sems

    def bind(self, acc, full, scratch):
        self.acc, self.full = acc, full
        self.slots = (scratch[:3], scratch[3:6])
        self.send, self.recv = scratch[6:]
        self.me = lax.axis_index("edge")
        self.begin = [0, self.rows // 2]
        self.length = [self.rows // 2] * 2
        self.flying = [[], []]
        self.used = 0

    def at(self, order, t):
        k, stride = order
        mine = (self.me // stride) % k
        other = (mine + t) % k
        return mine, other, self.me + (other - mine) * stride

    def peers(self):
        return [self.at(d, t)[2] for d in self.orders[0] for t in range(1, d[0])]

    def copy(self, source, target, device):
        out = pltpu.make_async_remote_copy(
            src_ref=source,
            dst_ref=target,
            send_sem=self.send.at[self.used],
            recv_sem=self.recv.at[self.used],
            device_id={"edge": device},
            device_id_type=pl.DeviceIdType.MESH,
        )
        self.used += 1
        out.start()
        return out

    def window(self, begin, length):
        return pl.ds(pl.multiple_of(begin, 8), length)

    def scatter(self, half, stage):
        side = self.orders[half][stage]
        k = side[0]
        length = self.length[half] // k
        for t in range(1, k):
            _, other, device = self.at(side, t)
            source = self.acc.at[self.window(self.begin[half] + other * length, length)]
            self.flying[half].append(self.copy(source, self.slots[half][stage].at[t - 1], device))
        self.begin[half] = self.begin[half] + ((self.me // side[1]) % k) * length
        self.length[half] = length

    def add(self, half, stage):
        for one in self.flying[half]:
            one.wait()
        self.flying[half] = []
        rows = self.window(self.begin[half], self.length[half])
        k = self.orders[half][stage][0]
        value = self.acc[rows, :]
        for t in range(1, k):
            value = value + self.slots[half][stage][t - 1]
        self.acc[rows, :] = value
        if stage == 2:
            self.full[rows, :] = value

    def gather(self, half, stage):
        side = self.orders[half][stage]
        k = side[0]
        rows = self.window(self.begin[half], self.length[half])
        for t in range(1, k):
            part = self.full.at[rows]
            self.flying[half].append(self.copy(part, part, self.at(side, t)[2]))

    def arrive(self, half, stage):
        for one in self.flying[half]:
            one.wait()
        self.flying[half] = []
        k, stride = self.orders[half][stage]
        self.begin[half] = self.begin[half] - ((self.me // stride) % k) * self.length[half]
        self.length[half] = self.length[half] * k

    def run(self):
        for stage in range(3):
            for half in range(2):
                if stage:
                    self.add(half, stage - 1)
                self.scatter(half, stage)
        for stage in (2, 1, 0):
            for half in range(2):
                if stage == 2:
                    self.add(half, 2)
                else:
                    self.arrive(half, stage + 1)
                self.gather(half, stage)
        for half in range(2):
            self.arrive(half, 0)


def reduce_kernel(reducer, mats, *refs):
    pieces, refs = refs[:4], refs[4:]
    rows_in, refs = refs[:4], refs[4:]
    errors, factors, refs = refs[0], refs[1], refs[2:]
    total_ref, left_ref, right_ref, small_ref, refs = *refs[:4], refs[4:]
    acc, full, mine, theirs, right_mine, right_theirs, pair_send, pair_recv = refs[:8]
    reducer.bind(acc, full, refs[8:])
    sibling = {"rep": 1 - lax.axis_index("rep")}
    barrier = pltpu.get_barrier_semaphore()
    peers = [{"edge": one} for one in reducer.peers()] + [sibling]
    for peer in peers:
        pl.semaphore_signal(barrier, inc=1, device_id=peer, device_id_type=pl.DeviceIdType.MESH)
    pl.semaphore_wait(barrier, len(peers))

    for ref, places in zip(pieces, PLACES):
        for i, place in enumerate(places):
            acc[place * LAT : (place + 1) * LAT, :] = ref[i]
    base = mats * LAT
    for ref, at in zip(rows_in, SMALL.values()):
        acc[base + at : base + at + ref.shape[0], :] = ref[...]
    acc[base + SMALL_ROWS :, :] = jnp.zeros((acc.shape[0] - base - SMALL_ROWS, LAT), F32)
    rank = factors.shape[1]

    def of(k):
        return pl.ds(pl.multiple_of(k * LAT, LAT), LAT)

    def ranked(k, offset=0):
        return pl.ds(pl.multiple_of(offset + k * rank, 8), rank)

    reducer.run()

    def project(k, unused):
        mine[ranked(k), :] = mm3(factors[k], full[of(k), :], NT)
        mine[ranked(k, mats * rank), :] = mm3(factors[k], errors[k], NT)
        return unused

    lax.fori_loop(0, mats, project, 0)
    end = 2 * mats * rank
    mine[end:, :] = full[base : base + SMALL_ROWS, :]

    def swap(source, target, at):
        one = pltpu.make_async_remote_copy(
            src_ref=source,
            dst_ref=target,
            send_sem=pair_send.at[at],
            recv_sem=pair_recv.at[at],
            device_id=sibling,
            device_id_type=pl.DeviceIdType.MESH,
        )
        one.start()
        one.wait()

    swap(mine, theirs, 0)
    small = mine[end:, :] + theirs[end:, :]
    small_ref[...] = small
    at = SMALL["sums"] + 10
    scale = 1.0 / jnp.sum(small[at : at + 1, :], 1, keepdims=True)
    half = mats * rank
    both = (mine[0:half, :] + theirs[0:half, :]) * scale
    both = both + (mine[half:end, :] + theirs[half:end, :])
    both = both.reshape(mats, rank, LAT)
    columns = [both[:, i, :] for i in range(rank)]
    for i in range(rank):
        v = columns[i]
        v = v * lax.rsqrt(jnp.sum(v * v, 1, keepdims=True) + 1e-12)
        columns[i] = v
        for j in range(i + 1, rank):
            columns[j] = columns[j] - jnp.sum(v * columns[j], 1, keepdims=True) * v
    for i in range(rank):
        left_ref[:, i, :] = columns[i]

    def transform(k, unused):
        total = full[of(k), :] * scale + errors[k]
        total_ref[k] = total
        right_mine[ranked(k), :] = mm3(left_ref[k], total)
        return unused

    lax.fori_loop(0, mats, transform, 0)
    swap(right_mine, right_theirs, 1)
    right_ref[...] = (right_mine[...] + right_theirs[...]).reshape(mats, rank, LAT)


def reduce_gradients(pieces, rows, errors, factors):
    mats, _, rank = factors.shape
    count = lax.axis_size("edge")
    unit = 16 * count
    height = -(-(mats * LAT + SMALL_ROWS) // unit) * unit
    reducer = Reducer(count, height)
    flat = lambda n: pltpu.VMEM((n, LAT), F32)
    message = 2 * mats * rank + SMALL_ROWS
    vmem = pl.BlockSpec(memory_space=pltpu.VMEM)
    shape = lambda *dims: jax.ShapeDtypeStruct(dims, F32)
    return pl.pallas_call(
        partial(reduce_kernel, reducer, mats),
        in_specs=[vmem] * 10,
        out_specs=[vmem] * 4,
        out_shape=[
            shape(mats, LAT, LAT), shape(mats, rank, LAT), shape(mats, rank, LAT),
            shape(SMALL_ROWS, LAT),
        ],
        scratch_shapes=[
            flat(height), flat(height), flat(message), flat(message), flat(mats * rank),
            flat(mats * rank), pltpu.SemaphoreType.DMA((2,)), pltpu.SemaphoreType.DMA((2,)),
        ]
        + reducer.scratch(),
        compiler_params=pltpu.CompilerParams(
            collective_id=0, has_side_effects=True, vmem_limit_bytes=56 << 20
        ),
    )(*pieces, *rows, errors, jnp.swapaxes(factors, 1, 2))


def finish_kernel(total, left, right, mats, momentum, new_mats, new_momentum, new_errors):
    for k in range(total.shape[0]):
        approx = mm3(left[k], right[k], TN)
        moved = 0.9 * momentum[k] + approx
        new_momentum[k] = moved
        new_mats[k] = mats[k] - 4.0 * moved
        new_errors[k] = total[k] - approx


def finish(total, left, right, mats, momentum):
    group = 4
    big = pl.BlockSpec((group, LAT, LAT), lambda i: (i, 0, 0))
    thin = pl.BlockSpec((group,) + left.shape[1:], lambda i: (i, 0, 0))
    return pl.pallas_call(
        finish_kernel,
        grid=(total.shape[0] // group,),
        in_specs=[big, thin, thin, big, big],
        out_specs=[big] * 3,
        out_shape=[jax.ShapeDtypeStruct(total.shape, F32)] * 3,
    )(total, left, right, mats, momentum)


def shards(
    node_feat, node_types, boundary, target, edge_feat, senders, receivers, edge_counts, mats, vecs,
    mats_momentum, vecs_momentum, factors, errors,
):
    own = node_feat.shape[1]
    wide = 3 * own
    count = senders.shape[1]
    place = lax.axis_index("edge")
    slots = jnp.arange(count, dtype=jnp.int32)
    live = slots < edge_counts[0, 0]
    send = senders[0] - (place - 1) * own
    recv = receivers[0] - place * own
    upper_s = send >= wide // 2
    upper_r = recv >= own // 2
    send = jnp.where(upper_s, send - wide // 2, send)
    recv = jnp.where(upper_r, recv - own // 2, recv)
    code = (send << 12) + jnp.where(upper_s, 2048, 0) + jnp.where(upper_r, 1024, 0) + recv
    code = jnp.where(live, code, (1023 << 12) + 1023).reshape(count // LAT, LAT)

    feat = jnp.concatenate(
        [node_feat[0].T, node_types.astype(F32), jnp.zeros((1, own), F32)], 0
    )
    from_left, from_right = shifted(feat, feat)
    feat_wide = jnp.concatenate([from_left, feat, from_right], 1)
    keep = (1 - boundary).astype(F32)
    goal = target[0].T
    x = edge_feat[0]

    kept_outs = [((count, LAT), kind, edges(LAT)) for kind in KINDS]
    vec_in = (vecs, whole(vecs.shape))
    mat = lambda at: (mats, third(at))
    node = (own, LAT)
    pairs = lambda n: pltpu.VMEM((n, LAT, LAT), BF16)
    tables = [
        pltpu.VMEM((2, wide // 2, 2 * LAT), BF16),
        pltpu.VMEM((2, own // 2, 2 * LAT), BF16),
        pltpu.VMEM((own // 2, 2 * LAT), F32),
    ]

    e0, *enc = call(
        encode_edges_kernel,
        count,
        [(x, edges(EFEAT)), mat(0), mat(1), vec_in],
        [((count, LAT), BF16, edges(LAT))] + kept_outs,
        [pairs(4)],
    )
    e1, *rest = call(
        partial(forward_first_kernel, own),
        count,
        [(code, CODE), (e0, edges(LAT)), (feat_wide, whole(feat_wide.shape)), mat(0)]
        + [mat(2), mat(3), mat(4), mat(5), vec_in],
        [((count, LAT), BF16, edges(LAT))]
        + kept_outs
        + [full((wide, LAT)), full((KEPT, wide, LAT)), full(node), full((KEPT,) + node)]
        + [full(node), full(node), full(node)],
        [pairs(6)] + tables,
    )
    kept0, rest = rest[:KEPT], rest[KEPT:]
    h0w, node_kept, agg0, upd_kept, h1, hb, hc = rest
    left, right = shifted(hb, hb)
    nodes = lambda v: (v, whole(v.shape))
    *kept1, dh, dagg, gm_n1, gv_n1, sums = call(
        partial(forward_second_kernel, own),
        count,
        [(code, CODE), (e1, edges(LAT)), nodes(left), nodes(hb), nodes(right), nodes(hc), nodes(h1)]
        + [mat(5), mat(6), mat(7), mat(1), vec_in, nodes(goal), nodes(keep), nodes(feat)],
        kept_outs
        + [full(node), full(node), full((6, LAT, LAT)), full((16, LAT)), full((16, LAT))],
        [pairs(6)] + tables,
    )
    totals = [
        pltpu.VMEM((own // 2, 2 * LAT), F32),
        pltpu.VMEM((wide // 2, 2 * LAT), F32),
    ]
    dagg_table = pltpu.VMEM((2, own // 2, 2 * LAT), BF16)
    row_sums = pltpu.VMEM((5, 8, LAT), F32)
    de, gm_e1, gv_e1, spread, s_recv = call(
        partial(backward_second_kernel, own),
        count,
        [(code, CODE)] + [(v, edges(LAT)) for v in kept1] + [(e1, edges(LAT)), nodes(dagg)]
        + [mat(5), mat(6), vec_in],
        [((count, LAT), BF16, edges(LAT)), full((3, LAT, LAT)), full((8, LAT)), full((wide, LAT))]
        + [full(node)],
        [pairs(6), dagg_table, row_sums] + totals,
    )
    from_left, from_right = shifted(spread[2 * own :], spread[:own])
    gm_e0, gm_n0, gv_0 = call(
        partial(backward_first_kernel, own),
        count,
        [(code, CODE)] + [(v, edges(LAT)) for v in kept0] + [(e0, edges(LAT))]
        + [(v, edges(LAT)) for v in enc] + [(x, edges(EFEAT)), (de, edges(LAT)), nodes(dh)]
        + [nodes(spread[own : 2 * own]), nodes(from_left), nodes(from_right), nodes(s_recv)]
        + [nodes(h1), nodes(h0w), nodes(node_kept), nodes(upd_kept), nodes(agg0), nodes(feat_wide)]
        + [mat(0), mat(1), mat(2), mat(3), mat(4), mat(5), vec_in],
        [full((5, LAT, LAT)), full((10, LAT, LAT)), full((48, LAT))],
        [pairs(10), dagg_table, row_sums, row_sums, pltpu.VMEM((EFEAT, LAT), F32)]
        + [pltpu.VMEM(node, F32)] + totals,
    )
    total, left, right, small = reduce_gradients(
        (gm_n1, gm_e1, gm_e0, gm_n0), (gv_n1, gv_e1, gv_0, sums), errors[0], factors
    )
    new_mats, mats_mom, new_errors = finish(total, left, right, mats, mats_momentum)
    sums = jnp.sum(small[SMALL["sums"] :][:12].reshape(6, 2, LAT), -1)
    kept_count = sums[5, 0]
    stats = sums[1:5] / kept_count
    n1, e1, n0 = (small[SMALL[name] :] for name in ("n1", "e1", "n0"))
    vec_grad = jnp.concatenate(
        [n0[23:46], n0[15:18], n0[18:23], n0[10:15], n0[5:10], n0[0:5], e1[0:5], n1[0:9]]
    )
    vecs_mom = 0.9 * vecs_momentum + vec_grad / kept_count
    return (
        sums[0, 0] + sums[0, 1],
        kept_count,
        stats,
        new_mats,
        mats_mom,
        jnp.swapaxes(right, 1, 2),
        new_errors[None],
        vecs - 4.0 * vecs_mom,
        vecs_mom,
    )


def solution(mesh):
    placed = (
        P("rep", "edge", None),
        P("rep", "edge"),
        P("rep", "edge"),
        P("rep", "edge", None),
        P("rep", "edge", None),
        P("rep", "edge"),
        P("rep", "edge"),
        P("rep", "edge"),
        P(),
        P(),
        P(),
        P(),
        P(),
        P("rep", None, None, None),
    )
    return jax.shard_map(
        shards,
        mesh=mesh,
        in_specs=placed,
        out_specs=(P(), P(), P(), P(), P(), P(), P("rep", None, None, None), P(), P()),
        check_vma=False,
    )
```

time: 1270 us -> 287 us (0.23)
  matrix products: 826 us -> 0 us
  Pallas kernels: 0 us -> 223 us
  blocking collectives: 122 us -> 0 us
  waiting for transfers between devices: 129 us -> 19.1 us
  local copies, waits for them, and re-layouts: 79.6 us -> 13 us
  other arithmetic: 57.8 us -> 6.95 us
  between operations: 16.9 us -> 3.91 us
    dot_general x276 -> x0, matrix products: 826 us -> none  [the longest x177 526 us: product(): return jnp.dot(a, b, precision=HIGH)]
    pallas_call x0 -> x7, Pallas kernels: none -> 223 us  [the longest x5 148 us: call(): pl.pallas_call(kernel, grid=(count // BLOCK,), in_specs=[spec for _, spec...]
    psum x3 -> x0, waiting for transfers between devices: 122 us -> none  [the longest x1 109 us: shards(): grad_m, grad_v = lax.psum((grad_m + part_m, grad_v + part_v), 'edge')]
    psum x3 -> x0, blocking collectives: 122 us -> none  [the longest x1 75.2 us: shards(): grad_m, grad_v = lax.psum((grad_m + part_m, grad_v + part_v), 'edge')]
    reduce_sum x36 -> x1, other arithmetic: 32.9 us -> 0.81 us  [shards(): sums = jnp.sum(small[SMALL['sums']:][:12].reshape(6, 2, LAT), -1)]
    dynamic_slice x192 -> x0, local copies, waits for them, and re-layouts: 24.4 us -> none  [pick_rows(): picked = lax.map(pick_one_block, index.reshape(count // size, size))]
    another operation x8 -> x0, local copies, waits for them, and re-layouts: 17.4 us -> none
    unnamed x321 -> x22, local copies, waits for them, and re-layouts: 22.4 us -> 6.96 us
  transfers between devices with their start and end apart: 11 -> 6, of which waited for: 4 -> 4; matrix products, arithmetic and copies ran while one was open for 14% -> 2% of each run, Pallas kernels for 0% -> 4%
where the time goes in v1:
time: 287 us; the launch traced here: 286 us
  Pallas kernels  223 us (78%)
  starting transfers between devices  20.1 us (7%)
  waiting for transfers between devices  19.1 us (7%)
  local copies, waits for them, and re-layouts  13 us (5%)
  other arithmetic  6.95 us (2%)
  between operations  3.91 us (1%)
    pallas_call x5, Pallas kernels, call(): pl.pallas_call(kernel, grid=(count // BLOCK,), in_specs=[spec for _, spec...  148 us
    pallas_call x1, Pallas kernels, reduce_gradients(): pl.pallas_call(partial(reduce_kernel, reducer, mats), in_specs=[vmem] * 1...  68.5 us
    ppermute x3, starting transfers between devices, shifted(): from_left = lax.ppermute(up, 'edge', [(i, i + 1) for i in range(ends)])  16.3 us
    ppermute x3, waiting for transfers between devices, shifted(): from_left = lax.ppermute(up, 'edge', [(i, i + 1) for i in range(ends)])  9.87 us
    ppermute x3, waiting for transfers between devices, shifted(): from_right = lax.ppermute(down, 'edge', [(i + 1, i) for i in range(ends)])  9.2 us
    unnamed x22, local copies, waits for them, and re-layouts  6.96 us
    pallas_call x1, Pallas kernels, finish(): pl.pallas_call(finish_kernel, grid=(total.shape[0] // group,), in_specs=[...  6.78 us
  transfers between devices with their start and end apart: 6, of which 4 were waited for; matrix products, arithmetic and copies ran while one was open for 2% of the time, Pallas kernels for 4%

profile of v1, /device:TPU:0, one launch (start us, length us, event | category | flops | bytes accessed | tf_op | source)
XLA Modules:
  0.0 286.1 jit_solution(7410526224874190469)
XLA Ops:
  0.6 0.7 convert_element_type.6
  1.3 0.8 copy.29
  2.1 0.0 copy-start.6
  2.1 1.3 collective-permute-start.1
  3.4 5.5 %collective-permute-start = (f32[16,512]{1,0:T(8,128)S(1)}, f32[16,512]{1,0:T(8,128)S(1)}, u32[]{:S(2)}, u32[]{:S(2)}) collective-permute-start(f32[16,512]{1,0:T(8,128)S(1)} %pad_maximum_fusion.1.feat_ref), channel_id=1, source_target_pairs={{0,2},{2,4},{4,6},{6,8},{8,10},{10,12},{12,14},{14,16},{16,18},{18... | collective-permute-start | bytes 98312 | tf_op jit(solution)/shard_map/ppermute | solution.py:547
  9.5 0.8 broadcast_subtract_fusion.1
  10.3 0.8 broadcast_subtract_fusion
  11.1 0.6 fusion.3.code_ref
  11.8 3.5 %copy.25 = f32[1,8192,3]{2,1,0:T(8,128)} copy(f32[1,8192,3]{1,0,2:T(1,128)} %param.18) | data formatting | bytes 196608 | tf_op args[4]
  15.2 0.0 copy-done.6
  15.2 12.9 %shard_map.205 = (bf16[8192,128]{1,0:T(8,128)(2,1)}, bf16[8192,128]{1,0:T(8,128)(2,1)}, f32[8192,128]{1,0:T(8,128)}, bf16[8192,128]{1,0:T(8,128)(2,1)}, f32[8192...) custom-call(f32[8192,3]{1,0:T(8,128)} %bitcast.19, f32[24,128,128]{2,1,0:T(8,128)} %mats.1, ...), custom_call_target="tpu_custom_call" | custom-call | tf_op jit(solution)/shard_map/pallas_call | solution.py:527
  28.1 0.0 collective-permute-done.1
  28.1 0.0 collective-permute-done
  28.1 0.7 pad_maximum_fusion.feat_ref.rest_25_
  28.8 0.0 copy-start.8
  28.8 38.8 %shard_map.206 = (bf16[8192,128]{1,0:T(8,128)(2,1)}, bf16[8192,128]{1,0:T(8,128)(2,1)}, f32[8192,128]{1,0:T(8,128)}, bf16[8192,128]{1,0:T(8,128)(2,1)}, f32[8192...) custom-call(s32[64,128]{1,0:T(8,128)} %fusion.3.code_ref, ...), custom_call_target="tpu_custom_call" | custom-call | tf_op jit(solution)/shard_map/pallas_call | solution.py:527
  67.6 1.3 collective-permute-start.3
  68.9 5.6 %collective-permute-start.2 = (f32[512,128]{1,0:T(8,128)}, f32[512,128]{1,0:T(8,128)S(1)}, u32[]{:S(2)}, u32[]{:S(2)}) collective-permute-start(f32[512,128]{1,0:T(8,128)} %get-tuple-element.58.mid), channel_id=1, source_target_pairs={{0,2},{2,4},{4,6},{6,8},{8,10},{10,12},{12,14},{14,16},{16,18},{18... | collective-permute-start | bytes 786440 | tf_op jit(solution)/shard_map/ppermute | solution.py:547
  74.5 0.0 copy-done.8
  74.6 0.6 subtract_convert_fusion.keep_ref
  75.1 4.5 %collective-permute-done.3.right = f32[512,128]{1,0:T(8,128)S(1)} collective-permute-done((f32[512,128]{1,0:T(8,128)}, f32[512,128]{1,0:T(8,128)S(1)}, u32[]{:S(2)}, u32[]{:S(2)}) %collective-permute-start.3) | collective-permute-done | bytes 262176 | tf_op jit(solution)/shard_map/ppermute | solution.py:548
  79.6 0.0 copy-start.4
  79.6 5.6 %collective-permute-done.2.left = f32[512,128]{1,0:T(8,128)S(1)} collective-permute-done((f32[512,128]{1,0:T(8,128)}, f32[512,128]{1,0:T(8,128)S(1)}, u32[]{:S(2)}, u32[]{:S(2)}) %collective-permute-start.2) | collective-permute-done | bytes 262176 | tf_op jit(solution)/shard_map/ppermute | solution.py:547
  85.3 0.0 copy-start.5
  85.3 0.0 copy-done.4
  85.3 0.7 copy-done.5
  86.0 36.2 %shard_map.207 = (bf16[8192,128]{1,0:T(8,128)(2,1)}, f32[8192,128]{1,0:T(8,128)}, bf16[8192,128]{1,0:T(8,128)(2,1)}, f32[8192,128]{1,0:T(8,128)}, bf16[8192,128]...) custom-call(s32[64,128]{1,0:T(8,128)} %fusion.3.code_ref, ...), custom_call_target="tpu_custom_call" | custom-call | tf_op jit(solution)/shard_map/pallas_call | solution.py:527
  122.2 22.8 %shard_map.208 = (bf16[8192,128]{1,0:T(8,128)(2,1)}, f32[3,128,128]{2,1,0:T(8,128)}, f32[8,128]{1,0:T(8,128)}, f32[1536,128]{1,0:T(8,128)}, f32[512,128]{1,0:T(8,128)}) custom-call(s32[64,128]{1,0:T(8,128)} %fusion.3.code_ref, bf16[8192,128]{1,0:T(8,128)(2,1)} %get-tuple-element.62.rest_0_, f32[8192,128]{1,0:T(8,128)} %get-tuple-element.63.rest_1_, ...), custom_call_target="tpu_custom_call" | custom-call | tf_op jit(solution)/shard_map/pallas_call | solution.py:527
  145.1 1.9 fusion.5
  146.9 1.3 collective-permute-start.5
  148.2 5.1 %collective-permute-start.4 = (f32[512,128]{1,0:T(8,128)S(1)}, f32[512,128]{1,0:T(8,128)S(1)}, u32[]{:S(2)}, u32[]{:S(2)}) collective-permute-start(f32[512,128]{1,0:T(8,128)S(1)} %get-tuple-element.124), channel_id=1, source_target_pairs={{0,2},{2,4},{4,6},{6,8},{8,10},{10,12},{12,14},{14,16},{16,18},{18... | collective-permute-start | bytes 786440 | tf_op jit(solution)/shard_map/ppermute | solution.py:547
  153.4 4.7 %collective-permute-done.5.rest_18_ = f32[512,128]{1,0:T(8,128)S(1)} collective-permute-done((f32[512,128]{1,0:T(8,128)S(1)}, f32[512,128]{1,0:T(8,128)S(1)}, u32[]{:S(2)}, u32[]{:S(2)}) %collective-permute-start.5) | collective-permute-done | bytes 262176 | tf_op jit(solution)/shard_map/ppermute | solution.py:548
  158.1 0.0 copy-start.2
  158.1 4.2 %collective-permute-done.4.rest_17_ = f32[512,128]{1,0:T(8,128)S(1)} collective-permute-done((f32[512,128]{1,0:T(8,128)S(1)}, f32[512,128]{1,0:T(8,128)S(1)}, u32[]{:S(2)}, u32[]{:S(2)}) %collective-permute-start.4) | collective-permute-done | bytes 262176 | tf_op jit(solution)/shard_map/ppermute | solution.py:547
  162.3 0.0 copy-start.3
  162.3 0.0 copy-done.2
  162.3 0.7 copy-done.3
  163.0 37.0 %shard_map.209 = (f32[5,128,128]{2,1,0:T(8,128)}, f32[10,128,128]{2,1,0:T(8,128)}, f32[48,128]{1,0:T(8,128)}) custom-call(s32[64,128]{1,0:T(8,128)} %fusion.3.code_ref, bf16[8192,128]{1,0:T(8,128)(2,1)} %get-tuple-element.70.rest_0_, f32[8192,128]{1,0:T(8,128)} %get-tuple-element.71.rest_1_, bf16[8192,128]{1,0:T(8,128)(2,1)} %get-tuple-element.72.rest_2_, ...), custom_call_target="tpu_custom_call" | custom-call | tf_op jit(solution)/shard_map/pallas_call | solution.py:527
  200.1 0.0 copy-start
  200.1 0.0 copy-start.7
  200.1 68.5 %shard_map.210 = (f32[24,128,128]{2,1,0:T(8,128)}, f32[24,8,128]{2,1,0:T(8,128)}, f32[24,8,128]{2,1,0:T(8,128)}, f32[88,128]{1,0:T(8,128)}) custom-call(f32[6,128,128]{2,1,0:T(8,128)} %get-tuple-element.61.refs_0_, f32[3,128,128]{2,1,0:T(8,128)} %get-tuple-element.69.refs_1_, f32[5,128,128]{2,1,0:T(8,128)} %get-tuple-element.90.refs_2_, ...), custom_call_target="tpu_custom_call" | custom-call | tf_op jit(solution)/shard_map/pallas_call | solution.py:770
  268.6 0.8 slice_reduce_fusion
  269.4 0.7 slice.74
  270.1 0.7 slice.79
  270.8 0.7 slice.73
  271.5 0.8 fusion.6
  272.3 0.1 reduce_sum.12
  272.4 0.6 fusion.7
  273.0 0.7 slice_divide_fusion
  273.7 0.1 div.17
  273.8 0.7 copy.26
  275.7 0.5 concatenate.12
  276.2 0.0 copy-done
  276.2 0.0 copy-done.7
  276.2 1.3 multiply_subtract_fusion
  277.5 0.0 copy-start.1
  277.5 6.8 %shard_map.211 = (f32[24,128,128]{2,1,0:T(8,128)}, f32[24,128,128]{2,1,0:T(8,128)}, f32[24,128,128]{2,1,0:T(8,128)}) custom-call(f32[24,128,128]{2,1,0:T(8,128)} %get-tuple-element.97.total, f32[24,8,128]{2,1,0:T(8,128)} %get-tuple-element.98.left, f32[24,8,128]{2,1,0:T(8,128)} %get-tuple-element.99.right, f32[24,128,128]{2,1,0:T(8,128)} %mats.1, ...), custom_call_target="tpu_custom_call" | custom-call | tf_op jit(solution)/shard_map/pallas_call | solution.py:802
  284.3 0.0 copy-done.1
  284.3 0.6 copy.32
  (2 shorter events, 0.0 us)
Async XLA Ops:
  2.1 13.1 %copy-start.6 = (f32[16,512]{1,0:T(8,128)}, f32[16,512]{1,0:T(8,128)S(1)}, u32[]{:S(2)}) copy-start(f32[16,512]{1,0:T(8,128)S(1)} %pad_maximum_fusion.1.feat_ref) | copy-start | bytes 98308
  2.1 26.0 %collective-permute-start.1 = (f32[16,512]{1,0:T(8,128)S(1)}, f32[16,512]{1,0:T(8,128)S(1)}, u32[]{:S(2)}, u32[]{:S(2)}) collective-permute-start(f32[16,512]{1,0:T(8,128)S(1)} %pad_maximum_fusion.1.feat_ref), channel_id=1, source_target_pairs={{2,0},{4,2},{6,4},{8,6},{10,8},{12,10},{14,12},{16,14},{18,16},{20... | collective-permute-start | bytes 98312 | tf_op jit(solution)/shard_map/ppermute | solution.py:548
  3.4 24.7 %collective-permute-start = (f32[16,512]{1,0:T(8,128)S(1)}, f32[16,512]{1,0:T(8,128)S(1)}, u32[]{:S(2)}, u32[]{:S(2)}) collective-permute-start(f32[16,512]{1,0:T(8,128)S(1)} %pad_maximum_fusion.1.feat_ref), channel_id=1, source_target_pairs={{0,2},{2,4},{4,6},{6,8},{8,10},{10,12},{12,14},{14,16},{16,18},{18... | collective-permute-start | bytes 98312 | tf_op jit(solution)/shard_map/ppermute | solution.py:547
  28.8 45.8 %copy-start.8 = (s32[1,512]{1,0:T(1,128)S(1)}, s32[1,512]{1,0:T(1,128)}, u32[]{:S(2)}) copy-start(s32[1,512]{1,0:T(1,128)} %param.16) | copy-start | bytes 6148
  67.6 12.1 %collective-permute-start.3 = (f32[512,128]{1,0:T(8,128)}, f32[512,128]{1,0:T(8,128)S(1)}, u32[]{:S(2)}, u32[]{:S(2)}) collective-permute-start(f32[512,128]{1,0:T(8,128)} %get-tuple-element.58.mid), channel_id=1, source_target_pairs={{2,0},{4,2},{6,4},{8,6},{10,8},{12,10},{14,12},{16,14},{18,16},{20... | collective-permute-start | bytes 786440 | tf_op jit(solution)/shard_map/ppermute | solution.py:548
  68.9 16.4 %collective-permute-start.2 = (f32[512,128]{1,0:T(8,128)}, f32[512,128]{1,0:T(8,128)S(1)}, u32[]{:S(2)}, u32[]{:S(2)}) collective-permute-start(f32[512,128]{1,0:T(8,128)} %get-tuple-element.58.mid), channel_id=1, source_target_pairs={{0,2},{2,4},{4,6},{6,8},{8,10},{10,12},{12,14},{14,16},{16,18},{18... | collective-permute-start | bytes 786440 | tf_op jit(solution)/shard_map/ppermute | solution.py:547
  79.6 5.6 %copy-start.4 = (f32[512,128]{1,0:T(8,128)}, f32[512,128]{1,0:T(8,128)S(1)}, u32[]{:S(2)}) copy-start(f32[512,128]{1,0:T(8,128)S(1)} %collective-permute-done.3.right) | copy-start | bytes 786436
  85.3 0.7 copy-start.5
  146.9 11.1 %collective-permute-start.5 = (f32[512,128]{1,0:T(8,128)S(1)}, f32[512,128]{1,0:T(8,128)S(1)}, u32[]{:S(2)}, u32[]{:S(2)}) collective-permute-start(f32[512,128]{1,0:T(8,128)S(1)} %get-tuple-element.123), channel_id=1, source_target_pairs={{2,0},{4,2},{6,4},{8,6},{10,8},{12,10},{14,12},{16,14},{18,16},{20... | collective-permute-start | bytes 786440 | tf_op jit(solution)/shard_map/ppermute | solution.py:548
  148.2 14.1 %collective-permute-start.4 = (f32[512,128]{1,0:T(8,128)S(1)}, f32[512,128]{1,0:T(8,128)S(1)}, u32[]{:S(2)}, u32[]{:S(2)}) collective-permute-start(f32[512,128]{1,0:T(8,128)S(1)} %get-tuple-element.124), channel_id=1, source_target_pairs={{0,2},{2,4},{4,6},{6,8},{8,10},{10,12},{12,14},{14,16},{16,18},{18... | collective-permute-start | bytes 786440 | tf_op jit(solution)/shard_map/ppermute | solution.py:547
  158.1 4.2 %copy-start.2 = (f32[512,128]{1,0:T(8,128)}, f32[512,128]{1,0:T(8,128)S(1)}, u32[]{:S(2)}) copy-start(f32[512,128]{1,0:T(8,128)S(1)} %collective-permute-done.5.rest_18_) | copy-start | bytes 786436
  162.3 0.7 copy-start.3
  200.1 76.2 %copy-start = (f32[60,128]{1,0:T(8,128)S(1)}, f32[60,128]{1,0:T(8,128)}, u32[]{:S(2)}) copy-start(f32[60,128]{1,0:T(8,128)} %rest_32_.1) | copy-start | bytes 92164
  200.1 76.2 %copy-start.7 = (f32[60,128]{1,0:T(8,128)S(1)}, f32[60,128]{1,0:T(8,128)}, u32[]{:S(2)}) copy-start(f32[60,128]{1,0:T(8,128)} %param.25) | copy-start | bytes 92164
  277.5 6.8 %copy-start.1 = (f32[24,8,128]{2,1,0:T(8,128)S(1)}, f32[24,8,128]{2,1,0:T(8,128)}, u32[]{:S(2)}) copy-start(f32[24,8,128]{2,1,0:T(8,128)} %get-tuple-element.99.right) | copy-start | bytes 294916

commit v2 on v0

v2 whole, which is shorter than its diff:
```python
from functools import partial

import jax
import jax.numpy as jnp
from jax import lax
from jax.experimental import pallas as pl
from jax.experimental.pallas import tpu as pltpu
from jax.sharding import PartitionSpec as P

NFEAT = 14
NTYPES = 9
EFEAT = 3
LEAD = NFEAT + NTYPES
ROWS0 = LEAD + EFEAT
LAT = 128
BLOCK = 1024
SUB = 512
SHIFT = 12
F32 = jnp.float32
BF16 = jnp.bfloat16
MESH = pl.DeviceIdType.MESH
NN = (((1,), (0,)), ((), ()))
NT = (((1,), (1,)), ((), ()))
TN = (((0,), (0,)), ((), ()))


def mm(a, b, dims=NN):
    return lax.dot_general(a, b, dims, preferred_element_type=F32)


def split(w):
    hi = w.astype(BF16)
    return hi, (w - hi.astype(F32)).astype(BF16)


def twice(a):
    return jnp.concatenate([a, a], 1)


def stacked(w):
    return jnp.concatenate(split(w), 0)


def side_by_side(v):
    return jnp.concatenate(split(v), 1)


def joined(wide):
    return wide[:, :LAT] + wide[:, LAT:]


def mm3(a, b, dims=NN):
    ah, al = split(a)
    bh, bl = split(b)
    return mm(ah, bh, dims) + (mm(ah, bl, dims) + mm(al, bh, dims))


def silu_half(half):
    up = 1.0 + jnp.tanh(half)
    value = half * up
    sig = 0.5 * up
    return value, sig + value - value * sig


def mean_last(v):
    return jnp.mean(v, -1, keepdims=True)


def center(w):
    return w - mean_last(w)


def fold_rows(v):
    total = v[0:8]
    for i in range(8, v.shape[0], 8):
        total = total + v[i : i + 8]
    return total


def row_sum(v):
    return jnp.sum(fold_rows(v), 0, keepdims=True)


def unfold(v):
    return jnp.concatenate([v[:, :LAT], v[:, LAT:]], 0)


def together(parts):
    parts = list(parts)
    while parts:
        for part in list(parts):
            try:
                next(part)
            except StopIteration:
                parts.remove(part)


def node_tail(first, second, third, vec):
    b1, b2, b3, g, o = vec
    half1 = 0.5 * (first + b1)
    half2 = 0.5 * (mm3(silu_half(half1)[0], second) + b2)
    z = mm3(silu_half(half2)[0], third) + b3
    c = z - mean_last(z)
    inv = lax.rsqrt(mean_last(c * c) + 1e-05)
    xhat = c * inv
    return xhat * g + o, (half1, half2, xhat, jnp.broadcast_to(inv, xhat.shape))


def node_tail_back(d, kept, second, third, vec):
    half1, half2, xhat, inv = kept
    s1, d1 = silu_half(half1)
    s2, d2 = silu_half(half2)
    dy = d * vec[3]
    dz3 = inv * (dy - mean_last(dy) - xhat * mean_last(dy * xhat))
    dz2 = mm3(dz3, third, NT) * d2
    dz1 = mm3(dz2, second, NT) * d1
    rows = [row_sum(v) for v in (dz1, dz2, dz3, d * xhat, d)]
    return dz1, mm3(s1, dz2, TN), mm3(s2, dz3, TN), rows


def edge_tail(rows, half, kept, second, third, vec, ones):
    _, b2, b3, g, o = vec
    kept[0][rows, :] = half.astype(BF16)
    s1 = silu_half(half)[0].astype(BF16)
    half = mm(twice(s1), second) + 0.5 * b2
    yield
    kept[1][rows, :] = half.astype(BF16)
    s2 = silu_half(half)[0].astype(BF16)
    c = mm(twice(s2), third) + center(b3)
    yield
    inv = lax.rsqrt(mm((c * c).astype(BF16), ones) + 1e-05)
    xhat = c * inv
    kept[2][rows, :] = xhat.astype(BF16)
    kept[3][rows, :] = inv.astype(BF16)
    return xhat * g + o


def edge_tail_back(rows, d, kept, second, third, g, ones, grads, sums):
    xhat = kept[2][rows, :].astype(F32)
    inv = kept[3][rows, :].astype(F32)
    dx = d * xhat
    dc = inv * (d * g - xhat * mm((dx * g).astype(BF16), ones))
    dcb = dc.astype(BF16)
    for at, v in ((2, dc), (3, dx), (4, d)):
        sums[at] += fold_rows(v)
    yield
    s2, d2 = silu_half(kept[1][rows, :].astype(F32))
    dz2 = mm(twice(dcb), third) * d2
    grads[1][...] += mm(s2.astype(BF16), dcb, TN)
    sums[1] += fold_rows(dz2)
    dz2b = dz2.astype(BF16)
    yield
    s1, d1 = silu_half(kept[0][rows, :].astype(F32))
    dz1 = mm(twice(dz2b), second) * d1
    grads[0][...] += mm(s1.astype(BF16), dz2b, TN)
    sums[0] += fold_rows(dz1)
    yield
    return dz1


def finish_sums(sums):
    rows = [jnp.sum(sums[i], 0, keepdims=True) for i in range(5)]
    rows[2] = center(rows[2])
    return rows


def columns_of(code):
    parts = [
        jnp.transpose(jnp.broadcast_to(code[q : q + 1, :], (LAT, LAT))) for q in range(code.shape[0])
    ]
    return jnp.concatenate(parts, 0)


def pick_mask(column, count):
    lanes = lax.broadcasted_iota(jnp.int32, (column.shape[0], LAT), 1)
    return [jnp.where(column == lanes + LAT * j, 1.0, 0.0).astype(BF16) for j in range(count // LAT)]


def add_mask(row, count):
    down = lax.broadcasted_iota(jnp.int32, (count, LAT), 0)
    parts = [
        jnp.where(row[q : q + 1, :] == down, 1.0, 0.0).astype(BF16) for q in range(row.shape[0])
    ]
    return jnp.concatenate(parts, 1)


def halves(v, upper):
    return jnp.concatenate([jnp.where(upper, 0.0, v), jnp.where(upper, v, 0.0)], 1).astype(BF16)


def send_of(code):
    return code >> SHIFT


def recv_of(code):
    return code & ((1 << SHIFT) - 1)


def folded(index, half):
    return jnp.where(index >= half, index - half, index)


def sides_of(count):
    return {16: (2, 2, 4), 64: (4, 4, 4)}.get(count, (count, 1, 1))


class Reducer:
    def __init__(self, count, rows):
        sides = sides_of(count)
        strides = (1, sides[0], sides[0] * sides[1])
        dims = list(zip(sides, strides))
        self.orders = (dims, [dims[1], dims[0], dims[2]])
        unit = 16 * count
        self.rows = -(-rows // unit) * unit

    def scratch(self):
        shapes = {"acc": pltpu.VMEM((self.rows, LAT), F32), "full": pltpu.VMEM((self.rows, LAT), F32)}
        copies = 0
        for half, order in enumerate(self.orders):
            length = self.rows // 2
            for stage, (k, _) in enumerate(order):
                length //= k
                shapes[f"slot{half}{stage}"] = pltpu.VMEM((max(k - 1, 1), length, LAT), F32)
                copies += k - 1
        shapes["send"] = pltpu.SemaphoreType.DMA((2 * copies,))
        shapes["recv"] = pltpu.SemaphoreType.DMA((2 * copies,))
        return shapes

    def bind(self, refs):
        self.refs = refs
        self.acc, self.full = refs["acc"], refs["full"]
        me = lax.axis_index("edge")
        self.begin = []
        self.length = []
        self.sems = {}
        used = 0
        for half, order in enumerate(self.orders):
            begin = [half * (self.rows // 2)]
            length = [self.rows // 2]
            for k, stride in order:
                length.append(length[-1] // k)
                begin.append(begin[-1] + ((me // stride) % k) * length[-1])
            self.begin.append(begin)
            self.length.append(length)
            for stage, (k, stride) in enumerate(order):
                for t in range(1, k):
                    for phase in range(2):
                        mine = (me // stride) % k
                        other = (mine + t) % k
                        self.sems[half, stage, phase, t] = (used, other, me + (other - mine) * stride)
                        used += 1

    def peers(self):
        order = self.orders[0]
        return [
            self.sems[0, stage, 0, t][2] for stage in range(3) for t in range(1, order[stage][0])
        ]

    def window(self, begin, length):
        return pl.ds(pl.multiple_of(begin, 8), length)

    def copies(self, half, stage, phase):
        k = self.orders[half][stage][0]
        out = []
        for t in range(1, k):
            at, other, device = self.sems[half, stage, phase, t]
            length = self.length[half][stage + 1]
            if phase == 0:
                rows = self.window(self.begin[half][stage] + other * length, length)
                source, target = self.acc.at[rows], self.refs[f"slot{half}{stage}"].at[t - 1]
            else:
                rows = self.window(self.begin[half][stage + 1], length)
                source = target = self.full.at[rows]
            out.append(
                pltpu.make_async_remote_copy(
                    src_ref=source,
                    dst_ref=target,
                    send_sem=self.refs["send"].at[at],
                    recv_sem=self.refs["recv"].at[at],
                    device_id={"edge": device},
                    device_id_type=MESH,
                )
            )
        return out

    def start(self, half, stage, phase):
        for one in self.copies(half, stage, phase):
            one.start()

    def wait(self, half, stage, phase):
        for one in self.copies(half, stage, phase):
            one.wait()
        if phase:
            return
        rows = self.window(self.begin[half][stage + 1], self.length[half][stage + 1])
        value = self.acc[rows, :]
        for t in range(1, self.orders[half][stage][0]):
            value = value + self.refs[f"slot{half}{stage}"][t - 1]
        if stage == 2:
            self.full[rows, :] = value
        else:
            self.acc[rows, :] = value

    SEQUENCE = ((0, 0), (1, 0), (2, 0), (2, 1), (1, 1), (0, 1))
    STEPS = len(SEQUENCE) + 1

    def step(self, index):
        for half in range(2):
            if index:
                self.wait(half, *self.SEQUENCE[index - 1])
            if index < len(self.SEQUENCE):
                self.start(half, *self.SEQUENCE[index])


PLACES = (
    (4, 5, 20, 21, 22, 23),
    (15, 18, 19, 16, 17, 11, 12, 13, 14),
    (6, 9, 10, 2, 3, 7, 8, 0, 1),
)
ROWS1 = 32
ROWS2 = 8
ROWS3 = 48


class Refs(dict):
    def __getattr__(self, name):
        return self[name]


def train_kernel(reducers, names, mats_count, rank, *refs):
    r = Refs(zip(names, refs))
    groups = []
    for i, reducer in enumerate(reducers):
        mark = f"sum{i}_"
        reducer.bind({k[len(mark) :]: v for k, v in r.items() if k.startswith(mark)})
        groups.append(reducer)
    first, second, third = groups
    own = r.feat.shape[1]
    count = r.code.shape[0] * LAT
    me = lax.axis_index("edge")
    last = lax.axis_size("edge") - 1
    has_left, has_right = me > 0, me < last
    sibling = {"rep": 1 - lax.axis_index("rep")}
    mats, vecs = r.mats, r.vecs
    ones = jnp.full((LAT, LAT), 1.0 / LAT, BF16)
    middle = pl.ds(own, own)

    def rows_of(which):
        base = ROWS0 + 5 * which
        return [vecs[base + i : base + i + 1, :] for i in range(5)]

    @pl.when(me == 0)
    def _():
        r.feat_wide[0] = jnp.zeros(r.feat.shape, F32)
        r.hb[0:own, :] = jnp.zeros((own, LAT), F32)
        r.rims[0] = jnp.zeros((own, LAT), F32)

    @pl.when(me == last)
    def _():
        r.feat_wide[2] = jnp.zeros(r.feat.shape, F32)
        r.hb[2 * own :, :] = jnp.zeros((own, LAT), F32)
        r.rims[1] = jnp.zeros((own, LAT), F32)

    barrier = pltpu.get_barrier_semaphore()

    around = [lax.rem(me + shift, last + 1) for shift in (1, last)]
    others = [{"edge": one} for one in first.peers() + around] + [sibling]
    for peer in others:
        pl.semaphore_signal(barrier, inc=1, device_id=peer, device_id_type=MESH)
    pl.semaphore_wait(barrier, len(others))

    def neighbours(at, up, up_target, down, down_target):
        def one(index, source, target, shift):
            return pltpu.make_async_remote_copy(
                src_ref=source,
                dst_ref=target,
                send_sem=r.halo_send.at[at + index],
                recv_sem=r.halo_recv.at[at + index],
                device_id={"edge": me + shift},
                device_id_type=MESH,
            )

        return one(0, up, up_target, 1), one(1, down, down_target, -1)

    def start(pair):
        @pl.when(has_right)
        def _():
            pair[0].start()

        @pl.when(has_left)
        def _():
            pair[1].start()

    def wait(pair):
        @pl.when(has_right)
        def _():
            pair[0].wait_send()
            pair[1].wait_recv()

        @pl.when(has_left)
        def _():
            pair[1].wait_send()
            pair[0].wait_recv()

    feats = neighbours(0, r.feat, r.feat_wide.at[0], r.feat, r.feat_wide.at[2])
    start(feats)

    def loop(body, during=None):
        def step(i, unused):
            if during is not None:
                for index in range(Reducer.STEPS):

                    @pl.when(i == index)
                    def _():
                        during.step(index)

            base = pl.multiple_of(i * (BLOCK // LAT), BLOCK // LAT)
            code = r.code[pl.ds(base, BLOCK // LAT), :]
            per = count // LAT
            planes = [r.x[pl.ds(base + p * per, BLOCK // LAT), :] for p in range(EFEAT)]
            parts = []
            for at in range(0, BLOCK, SUB):
                rows = pl.ds(pl.multiple_of(i * BLOCK + at, SUB), SUB)
                cut = slice(at // LAT, (at + SUB) // LAT)
                parts.append(body(rows, code[cut], [plane[cut] for plane in planes]))
            together(parts)
            return unused

        lax.fori_loop(0, count // BLOCK, step, 0)

    def features(planes):
        lines = [
            jnp.concatenate([plane[q : q + 1, :] for q in range(plane.shape[0])], 1)
            for plane in planes
        ]
        return jnp.concatenate(lines, 0)

    kept = [[r[f"{name}{i}"] for i in range(4)] for name in ("enc", "one", "two")]

    r.w[0] = stacked(0.5 * mats[2])
    r.w[1] = stacked(center(mats[3]))
    vec = rows_of(1)

    def encode(rows, code, planes):
        half = mm3(features(planes), 0.5 * vecs[LEAD:ROWS0, :], TN) + 0.5 * vec[0]
        yield
        out = yield from edge_tail(rows, half, kept[0], r.w[0], r.w[1], vec, ones)
        r.e0[rows, :] = out.astype(BF16)

    loop(encode)

    r.feat_wide[1] = r.feat[...]
    wait(feats)
    def particle_inputs():
        lines = jnp.concatenate([r.feat_wide[i] for i in range(3)], 1)
        types = lax.broadcasted_iota(jnp.int32, (NTYPES, 3 * own), 0).astype(F32)
        return lines[0:NFEAT], jnp.where(lines[NFEAT : NFEAT + 1] == types, 1.0, 0.0)

    lines, onehot = particle_inputs()
    pre = mm3(lines, vecs[0:NFEAT, :], TN) + mm3(onehot, vecs[NFEAT:LEAD, :], TN)
    out, saved = node_tail(pre, mats[0], mats[1], rows_of(0))
    r.h0[...] = out
    for j, v in enumerate(saved):
        r.node_kept[j] = v
    r.table[0 : 3 * own, :] = side_by_side(0.5 * mm3(out, mats[7]))
    r.table[3 * own :, :] = side_by_side(0.5 * mm3(out[own : 2 * own], mats[8]))

    def forward(step, e_in, e_out):
        base = 6 + 9 * step
        vec = rows_of(2 + 2 * step)
        r.w[0] = stacked(0.5 * mats[base])
        r.w[1] = stacked(0.5 * mats[base + 3])
        r.w[2] = stacked(center(mats[base + 4]))
        r.agg_wide[...] = jnp.zeros_like(r.agg_wide)

        def body(rows, code, planes):
            column = columns_of(code)
            e = e_in[rows, :]
            mask = pick_mask(send_of(column), 3 * own) + pick_mask(recv_of(column), own)
            half = joined(mm(jnp.concatenate(mask, 1), r.table[...]))
            half = half + mm(twice(e), r.w[0]) + 0.5 * vec[0]
            yield
            out = yield from edge_tail(rows, half, kept[1 + step], r.w[1], r.w[2], vec, ones)
            if e_out is not None:
                e_out[rows, :] = (e.astype(F32) + out).astype(BF16)
            r.agg_wide[...] += mm(add_mask(recv_of(code), own), side_by_side(out))

        loop(body)

    forward(0, r.e0, r.e1)
    h = r.h0[middle, :]
    agg = joined(r.agg_wide[...])
    r.agg0[...] = agg
    delta, saved = node_tail(mm3(h, mats[11]) + mm3(agg, mats[12]), mats[13], mats[14], rows_of(3))
    for j, v in enumerate(saved):
        r.step_kept[j] = v
    h = h + delta
    r.h1[...] = h
    r.hb[middle, :] = 0.5 * mm3(h, mats[16])
    mine = r.hb.at[middle]
    latents = neighbours(2, mine, r.hb.at[pl.ds(0, own)], mine, r.hb.at[pl.ds(2 * own, own)])
    start(latents)
    r.table[3 * own :, :] = side_by_side(0.5 * mm3(h, mats[17]))
    r.table[middle, :] = side_by_side(r.hb[middle, :])
    wait(latents)
    for i in (0, 2):
        r.table[i * own : (i + 1) * own, :] = side_by_side(r.hb[i * own : (i + 1) * own, :])

    forward(1, r.e1, None)

    def slot(group, places, which):
        at = places.index(which) * LAT
        return group.acc.at[pl.ds(at, LAT)]

    def put(group, places, which, value):
        slot(group, places, which)[...] = value

    def put_rows(group, places, at, rows):
        base = len(places) * LAT + at
        for v in rows:
            group.acc[base : base + v.shape[0], :] = v
            base += v.shape[0]
        return base

    put1, put2, put3 = (partial(put, group, places) for group, places in zip(groups, PLACES))
    agg = joined(r.agg_wide[...])
    h = r.h1[...]
    vec = rows_of(5)
    delta, saved = node_tail(mm3(h, mats[20]) + mm3(agg, mats[21]), mats[22], mats[23], vec)
    out = h + delta
    base = ROWS0 + 30
    s1, d1 = silu_half(0.5 * (mm3(out, mats[4]) + vecs[base : base + 1, :]))
    s2, d2 = silu_half(0.5 * (mm3(s1, mats[5]) + vecs[base + 1 : base + 2, :]))
    ends = vecs[base + 2 : base + 4, :]
    keep = r.keep[...]
    goal = r.goal[...]
    diff = mm3(ends, s2, NT) - goal
    kept_diff = diff * keep
    dpred = 2.0 * kept_diff
    dz2 = mm3(dpred, ends, TN) * d2
    dz1 = mm3(dz2, mats[5], NT) * d1
    d = mm3(dz1, mats[4], NT)
    dz, g_second, g_third, rows = node_tail_back(d, saved, mats[22], mats[23], vec)
    r.dh[...] = d + mm3(dz, mats[20], NT)
    r.dagg[...] = side_by_side(mm3(dz, mats[21], NT))
    put1(4, mm3(out, dz1, TN))
    put1(5, mm3(s1, dz2, TN))
    put1(20, mm3(h, dz, TN))
    put1(21, mm3(agg, dz, TN))
    put1(22, g_second)
    put1(23, g_third)
    rows = rows + [row_sum(dz1), row_sum(dz2), mm3(dpred, s2)]
    rows.append(jnp.zeros((7, LAT), F32))
    velocity = r.feat[8:10, :]
    for v in (
        kept_diff * diff,
        velocity * keep,
        velocity * velocity * keep,
        goal * keep,
        goal * goal * keep,
        jnp.broadcast_to(keep, velocity.shape),
    ):
        part = v[:, 0:LAT]
        for j in range(LAT, own, LAT):
            part = part + v[:, j : j + LAT]
        rows.append(part)
    end = put_rows(first, PLACES[0], 0, rows)
    first.acc[end:, :] = jnp.zeros((first.rows - end, LAT), F32)

    def zero(*targets):
        for target in targets:
            target[...] = jnp.zeros_like(target)

    def backward(step, group, places, e_ref, more, during):
        base = 6 + 9 * step
        grads = [slot(group, places, which) for which in (base, base + 3, base + 4)]
        for i, w in enumerate((mats[base], mats[base + 3], center(mats[base + 4]))):
            r.w[i] = stacked(jnp.transpose(w))
        zero(*grads, r.sums, r.recv_total, r.send_total)
        vec = rows_of(2 + 2 * step)

        def body(rows, code, planes):
            column = columns_of(code)
            recv = recv_of(column)
            d = joined(mm(jnp.concatenate(pick_mask(recv, own), 1), r.dagg[...]))
            if more is not None:
                de = r.de[rows, :].astype(F32)
                d = d + de
            yield
            dz1 = yield from edge_tail_back(
                rows, d, kept[1 + step], r.w[1], r.w[2], vec[3], ones, grads[1:], r.sums
            )
            dz1b = dz1.astype(BF16)
            grads[0][...] += mm(e_ref[rows, :], dz1b, TN)
            half = own // 2
            r.recv_total[...] += mm(
                add_mask(folded(recv_of(code), half), half), halves(dz1, recv >= half)
            )
            half = 3 * half
            r.send_total[...] += mm(
                add_mask(folded(send_of(code), half), half), halves(dz1, column >= (half << SHIFT))
            )
            back = mm(twice(dz1b), r.w[0])
            if more is None:
                r.de[rows, :] = back.astype(BF16)
            else:
                yield from more(rows, planes, de + back)

        loop(body, during)
        grads[2][...] = center(grads[2][...])

    backward(1, second, PLACES[1], r.e1, None, first)
    end = put_rows(second, PLACES[1], 0, finish_sums(r.sums))
    second.acc[end:, :] = jnp.zeros((second.rows - end, LAT), F32)
    r.spread[...] = unfold(r.send_total[...])
    rims = neighbours(
        4, r.spread.at[pl.ds(2 * own, own)], r.rims.at[0], r.spread.at[pl.ds(0, own)], r.rims.at[1]
    )
    start(rims)
    got = unfold(r.recv_total[...])
    h = r.h1[...]
    put2(17, mm3(h, got, TN))
    d = r.dh[...] + mm3(got, mats[17], NT)
    wait(rims)
    sent = r.spread[middle, :] + r.rims[0] + r.rims[1]
    put2(16, mm3(h, sent, TN))
    d = d + mm3(sent, mats[16], NT)
    saved = [r.step_kept[j] for j in range(4)]
    dz, g_second, g_third, rows = node_tail_back(d, saved, mats[13], mats[14], rows_of(3))
    put2(11, mm3(r.h0[middle, :], dz, TN))
    put2(12, mm3(r.agg0[...], dz, TN))
    put2(13, g_second)
    put2(14, g_third)
    put_rows(third, PLACES[2], 0, rows)
    r.dh[...] = d + mm3(dz, mats[11], NT)
    r.dagg[...] = side_by_side(mm3(dz, mats[12], NT))

    enc_grads = [slot(third, PLACES[2], which) for which in (2, 3)]
    zero(*enc_grads, r.enc_sums, r.we)
    r.w[3] = stacked(jnp.transpose(mats[2]))
    r.w[4] = stacked(jnp.transpose(center(mats[3])))

    def encoder_back(rows, planes, d):
        dz1 = yield from edge_tail_back(
            rows, d, kept[0], r.w[3], r.w[4], rows_of(1)[3], ones, enc_grads, r.enc_sums
        )
        r.we[...] += mm(features(planes).astype(BF16), dz1.astype(BF16))

    backward(0, third, PLACES[2], r.e0, encoder_back, second)
    enc_grads[1][...] = center(enc_grads[1][...])
    rows = finish_sums(r.sums) + finish_sums(r.enc_sums) + [r.we[...]]
    sent = unfold(r.send_total[...])
    got = unfold(r.recv_total[...])
    h = r.h0[...]
    put3(7, mm3(h, sent, TN))
    put3(8, mm3(h[own : 2 * own], got, TN))
    d = mm3(sent, mats[7], NT)
    inner = d[own : 2 * own] + r.dh[...] + mm3(got, mats[8], NT)
    d = jnp.concatenate([d[:own], inner, d[2 * own :]], 0)
    saved = [r.node_kept[j] for j in range(4)]
    dz, g_second, g_third, more = node_tail_back(d, saved, mats[0], mats[1], rows_of(0))
    put3(0, g_second)
    put3(1, g_third)
    lines, onehot = particle_inputs()
    rows = rows + more + [mm3(lines, dz), mm3(onehot, dz)]
    end = put_rows(third, PLACES[2], 5, rows)
    third.acc[end:, :] = jnp.zeros((third.rows - end, LAT), F32)

    def swap(at, source, target):
        return pltpu.make_async_remote_copy(
            src_ref=source,
            dst_ref=target,
            send_sem=r.pair_send.at[at],
            recv_sem=r.pair_recv.at[at],
            device_id=sibling,
            device_id_type=MESH,
        )

    def gradient(which):
        for group, places in zip(groups, PLACES):
            if which in places:
                return group.full[places.index(which) * LAT : (places.index(which) + 1) * LAT, :]
        return None

    def ranked(which):
        return slice(which * rank, (which + 1) * rank)

    third.step(0)
    r.small_mine[0:ROWS1, :] = first.full[6 * LAT : 6 * LAT + ROWS1, :]
    r.small_mine[ROWS1:, :] = second.full[9 * LAT : 9 * LAT + ROWS2, :]
    small = swap(0, r.small_mine, r.small_theirs)
    small.start()
    early = PLACES[0] + PLACES[1]
    for which in range(mats_count):
        r.projected[ranked(which), :] = mm3(r.factors[which], r.errors[which], NT)
    third.step(1)
    small.wait()
    small = r.small_mine[...] + r.small_theirs[...]
    r.small[0 : ROWS1 + ROWS2, :] = small
    at = 16 + 10
    scale = 1.0 / jnp.sum(small[at : at + 1, :], 1, keepdims=True)
    for which in early:
        total = gradient(which) * scale + r.errors[which]
        r.total[which] = total
    third.step(2)
    for which in early:
        r.projected[ranked(which), :] += scale * mm3(r.factors[which], gradient(which), NT)
    for index in range(3, Reducer.STEPS):
        third.step(index)
    for which in PLACES[2]:
        part = gradient(which)
        r.total[which] = part * scale + r.errors[which]
        r.projected[ranked(which), :] += scale * mm3(r.factors[which], part, NT)
    end = mats_count * rank
    r.projected[end:, :] = third.full[9 * LAT : 9 * LAT + ROWS3, :]
    both = swap(1, r.projected, r.projected_theirs)
    both.start()
    both.wait()
    r.small[ROWS1 + ROWS2 :, :] = r.projected[end:, :] + r.projected_theirs[end:, :]
    both = (r.projected[0:end, :] + r.projected_theirs[0:end, :]).reshape(mats_count, rank, LAT)
    columns = [both[:, i, :] for i in range(rank)]
    for i in range(rank):
        v = columns[i]
        v = v * lax.rsqrt(jnp.sum(v * v, 1, keepdims=True) + 1e-12)
        columns[i] = v
        for j in range(i + 1, rank):
            columns[j] = columns[j] - jnp.sum(v * columns[j], 1, keepdims=True) * v
    for i in range(rank):
        r.left[:, i, :] = columns[i]
    for which in range(mats_count):
        r.right_mine[ranked(which), :] = mm3(r.left[which], r.total[which])
    both = swap(2, r.right_mine, r.right_theirs)
    both.start()
    both.wait()
    r.right[...] = (r.right_mine[...] + r.right_theirs[...]).reshape(mats_count, rank, LAT)


def train(inputs, count_edge):
    own = inputs["feat"].shape[1]
    count = inputs["code"].shape[0] * LAT
    mats_count, rank, _ = inputs["factors"].shape
    reducers = [
        Reducer(count_edge, len(places) * LAT + rows)
        for places, rows in zip(PLACES, (ROWS1, ROWS2, ROWS3))
    ]
    flat = lambda *dims: pltpu.VMEM(dims, F32)
    half = lambda *dims: pltpu.VMEM(dims, BF16)
    small = ROWS1 + ROWS2 + ROWS3
    outs = {
        "total": (mats_count, LAT, LAT),
        "left": (mats_count, rank, LAT),
        "right": (mats_count, rank, LAT),
        "small": (small, LAT),
    }
    scratch = {
        "feat_wide": flat(3, *inputs["feat"].shape),
        "w": half(5, 2 * LAT, LAT),
        "h0": flat(3 * own, LAT),
        "node_kept": flat(4, 3 * own, LAT),
        "step_kept": flat(4, own, LAT),
        "table": half(4 * own, 2 * LAT),
        "dagg": half(own, 2 * LAT),
        "agg_wide": flat(own, 2 * LAT),
        "agg0": flat(own, LAT),
        "h1": flat(own, LAT),
        "hb": flat(3 * own, LAT),
        "dh": flat(own, LAT),
        "spread": flat(3 * own, LAT),
        "rims": flat(2, own, LAT),
        "recv_total": flat(own // 2, 2 * LAT),
        "send_total": flat(3 * own // 2, 2 * LAT),
        "sums": flat(5, 8, LAT),
        "enc_sums": flat(5, 8, LAT),
        "we": flat(EFEAT, LAT),
        "e0": half(count, LAT),
        "e1": half(count, LAT),
        "de": half(count, LAT),
        "small_mine": flat(ROWS1 + ROWS2, LAT),
        "small_theirs": flat(ROWS1 + ROWS2, LAT),
        "projected": flat(mats_count * rank + ROWS3, LAT),
        "projected_theirs": flat(mats_count * rank + ROWS3, LAT),
        "right_mine": flat(mats_count * rank, LAT),
        "right_theirs": flat(mats_count * rank, LAT),
        "halo_send": pltpu.SemaphoreType.DMA((6,)),
        "halo_recv": pltpu.SemaphoreType.DMA((6,)),
        "pair_send": pltpu.SemaphoreType.DMA((3,)),
        "pair_recv": pltpu.SemaphoreType.DMA((3,)),
    }
    for name in ("enc", "one", "two"):
        for i in range(4):
            scratch[f"{name}{i}"] = half(count, LAT)
    for i, reducer in enumerate(reducers):
        for name, shape in reducer.scratch().items():
            scratch[f"sum{i}_{name}"] = shape
    vmem = pl.BlockSpec(memory_space=pltpu.VMEM)
    names = list(inputs) + list(outs) + list(scratch)
    return pl.pallas_call(
        partial(train_kernel, reducers, names, mats_count, rank),
        in_specs=[vmem] * len(inputs),
        out_specs=[vmem] * len(outs),
        out_shape=[jax.ShapeDtypeStruct(shape, F32) for shape in outs.values()],
        scratch_shapes=list(scratch.values()),
        compiler_params=pltpu.CompilerParams(
            collective_id=0, has_side_effects=True, vmem_limit_bytes=VMEM_LIMIT
        ),
    )(*inputs.values())


VMEM_LIMIT = 62 << 20


def finish_kernel(total, left, right, small, mats, momentum, vecs, vecs_momentum, *outs):
    new_mats, new_momentum, new_errors, new_vecs, new_vecs_momentum, loss, kept_count, stats = outs
    for k in range(total.shape[0]):
        approx = mm3(left[k], right[k], TN)
        moved = 0.9 * momentum[k] + approx
        new_momentum[k] = moved
        new_mats[k] = mats[k] - 4.0 * moved
        new_errors[k] = total[k] - approx

    @pl.when(pl.program_id(0) == 0)
    def _():
        sums = jnp.sum(small[16:28, :], 1, keepdims=True)
        kept = sums[10:11]
        scale = 1.0 / kept
        loss[...] = sums[0:1] + sums[1:2]
        kept_count[...] = kept
        stats[...] = sums[2:10] * scale
        late = ROWS1 + ROWS2
        cuts = (
            (late + 23, 23), (late + 15, 3), (late + 18, 5), (late + 10, 5), (late + 5, 5),
            (late, 5), (ROWS1, 5), (0, 9),
        )
        grads = jnp.concatenate([small[at : at + length, :] for at, length in cuts], 0)
        moved = 0.9 * vecs_momentum[...] + grads * scale
        new_vecs_momentum[...] = moved
        new_vecs[...] = vecs[...] - 4.0 * moved


def finish(total, left, right, small, mats, momentum, vecs, vecs_momentum):
    group = 6
    big = pl.BlockSpec((group, LAT, LAT), lambda i: (i, 0, 0))
    thin = pl.BlockSpec((group,) + left.shape[1:], lambda i: (i, 0, 0))
    whole = lambda shape: pl.BlockSpec(shape, lambda i: (0,) * len(shape))
    shape = lambda *dims: jax.ShapeDtypeStruct(dims, F32)
    return pl.pallas_call(
        finish_kernel,
        grid=(total.shape[0] // group,),
        in_specs=[big, thin, thin, whole(small.shape), big, big]
        + [whole(vecs.shape), whole(vecs.shape)],
        out_specs=[big] * 3 + [whole(vecs.shape)] * 2 + [whole((1, 1))] * 2 + [whole((8, 1))],
        out_shape=[shape(*total.shape)] * 3
        + [shape(*vecs.shape)] * 2
        + [shape(1, 1), shape(1, 1), shape(8, 1)],
    )(total, left, right, small, mats, momentum, vecs, vecs_momentum)


def shards(
    node_feat, node_types, boundary, target, edge_feat, senders, receivers, edge_counts, mats, vecs,
    mats_momentum, vecs_momentum, factors, errors,
):
    own = node_feat.shape[1]
    count = senders.shape[1]
    place = lax.axis_index("edge")
    lines = (count // LAT, LAT)
    slots = jnp.arange(count, dtype=jnp.int32).reshape(lines)
    send = senders.reshape(lines) - (place - 1) * own
    recv = receivers.reshape(lines) - place * own
    live = slots < edge_counts[0, 0]
    code = jnp.where(live, (send << SHIFT) + recv, (2047 << SHIFT) + 1023)
    feat = jnp.concatenate(
        [node_feat[0].T, node_types.astype(F32), jnp.zeros((1, own), F32)], 0
    )
    inputs = {
        "code": code,
        "x": edge_feat[0].T.reshape(EFEAT * lines[0], LAT),
        "feat": feat,
        "keep": (1 - boundary).astype(F32),
        "goal": target[0].T,
        "mats": mats,
        "vecs": vecs,
        "factors": jnp.swapaxes(factors, 1, 2),
        "errors": errors[0],
    }
    total, left, right, small = train(inputs, lax.axis_size("edge"))
    new_mats, mats_mom, new_errors, new_vecs, vecs_mom, loss, kept, stats = finish(
        total, left, right, small, mats, mats_momentum, vecs, vecs_momentum
    )
    return (
        loss.reshape(()),
        kept.reshape(()),
        stats.reshape(4, 2),
        new_mats,
        mats_mom,
        jnp.swapaxes(right, 1, 2),
        new_errors[None],
        new_vecs,
        vecs_mom,
    )


def solution(mesh):
    placed = (
        P("rep", "edge", None),
        P("rep", "edge"),
        P("rep", "edge"),
        P("rep", "edge", None),
        P("rep", "edge", None),
        P("rep", "edge"),
        P("rep", "edge"),
        P("rep", "edge"),
        P(),
        P(),
        P(),
        P(),
        P(),
        P("rep", None, None, None),
    )
    return jax.shard_map(
        shards,
        mesh=mesh,
        in_specs=placed,
        out_specs=(P(), P(), P(), P(), P(), P(), P("rep", None, None, None), P(), P()),
        check_vma=False,
    )
```

time: 1270 us -> 200 us (0.16)
  matrix products: 826 us -> 0 us
  Pallas kernels: 0 us -> 190 us
  waiting for transfers between devices: 129 us -> 0 us
  blocking collectives: 122 us -> 0 us
  local copies, waits for them, and re-layouts: 79.6 us -> 3.88 us
  other arithmetic: 57.8 us -> 4.89 us
  starting transfers between devices: 26.2 us -> 0 us
  between operations: 16.9 us -> 1.33 us
    dot_general x276 -> x0, matrix products: 826 us -> none  [the longest x177 526 us: product(): return jnp.dot(a, b, precision=HIGH)]
    pallas_call x0 -> x2, Pallas kernels: none -> 190 us  [the longest x1 184 us: train(): pl.pallas_call(partial(train_kernel, reducers, names, mats_count, rank),...]
    psum x3 -> x0, waiting for transfers between devices: 122 us -> none  [the longest x1 109 us: shards(): grad_m, grad_v = lax.psum((grad_m + part_m, grad_v + part_v), 'edge')]
    psum x3 -> x0, blocking collectives: 122 us -> none  [the longest x1 75.2 us: shards(): grad_m, grad_v = lax.psum((grad_m + part_m, grad_v + part_v), 'edge')]
    reduce_sum x36 -> x0, other arithmetic: 32.9 us -> none  [the longest x6 9.33 us: mlp_tail(): hidden = product(hidden, mats[third]) + vecs[base + 2]]
    ppermute x8 -> x0, starting transfers between devices: 26.1 us -> none  [the longest x4 20.5 us: extended(): lax.ppermute(tail, axis, [(i, (i + 1) % count) for i in range(ends)])]
    dynamic_slice x192 -> x0, local copies, waits for them, and re-layouts: 24.4 us -> none  [pick_rows(): picked = lax.map(pick_one_block, index.reshape(count // size, size))]
    unnamed x321 -> x6, local copies, waits for them, and re-layouts: 22.4 us -> 3.01 us
  transfers between devices with their start and end apart: 11 -> 0, of which waited for: 4 -> 0; matrix products, arithmetic and copies ran while one was open for 14% -> 0% of each run, Pallas kernels for 0% -> 0%
where the time goes in v2:
time: 200 us
  Pallas kernels  190 us (95%)
  other arithmetic  4.89 us (2%)
  local copies, waits for them, and re-layouts  3.88 us (2%)
    pallas_call x1, Pallas kernels, train(): pl.pallas_call(partial(train_kernel, reducers, names, mats_count, rank),...  184 us
    pallas_call x1, Pallas kernels, finish(): pl.pallas_call(finish_kernel, grid=(total.shape[0] // group,), in_specs=[...  5.84 us

profile of v2, /device:TPU:0, one launch (start us, length us, event | category | flops | bytes accessed | tf_op | source)
XLA Modules:
  0.0 200.0 jit_solution(17428162607261505156)
XLA Ops:
  0.6 0.8 subtract_add_fusion
  2.1 0.6 fusion.refs_0_
  2.7 1.0 copy.29
  3.7 0.7 reshape.49.refs_1_
  4.4 0.8 copy.30
  5.2 0.7 convert_element_type.6
  5.9 0.1 pad.2.clone
  5.9 0.7 maximum_maximum_fusion.refs_2_
  6.6 1.3 subtract_convert_fusion.refs_3_
  7.9 184.0 %shard_map.205 = (f32[24,128,128]{2,1,0:T(8,128)}, f32[24,8,128]{2,1,0:T(8,128)}, f32[24,8,128]{2,1,0:T(8,128)}, f32[88,128]{1,0:T(8,128)}) custom-call(s32[64,128]{1,0:T(8,128)} %fusion.refs_0_, f32[192,128]{1,0:T(8,128)} %reshape.49.refs_1_, f32[16,512]{1,0:T(8,128)} %maximum_maximum_fusion.refs_2_, f32[1,512]{1,0:T(1,128)} %subtract_convert_fusion.refs_3_, ...), custom_call_target="tpu_custom_call" | custom-call | tf_op jit(solution)/shard_map/pallas_call | solution.py:797
  191.9 0.0 copy-start
  191.9 5.8 %shard_map.206 = (f32[24,128,128]{2,1,0:T(8,128)}, f32[24,128,128]{2,1,0:T(8,128)}, f32[24,128,128]{2,1,0:T(8,128)}, f32[60,128]{1,0:T(8,128)}, f32[60,128]{1,0:...) custom-call(f32[24,128,128]{2,1,0:T(8,128)} %get-tuple-element.21.total, ...), custom_call_target="tpu_custom_call" | custom-call | tf_op jit(solution)/shard_map/pallas_call | solution.py:846
  197.8 0.8 reduce
  198.6 0.1 reshape.52
  198.7 0.7 copy.24
  199.3 0.0 copy-done
  199.3 0.6 copy.33
Async XLA Ops:
  191.9 7.4 %copy-start = (f32[24,8,128]{2,1,0:T(8,128)S(1)}, f32[24,8,128]{2,1,0:T(8,128)}, u32[]{:S(2)}) copy-start(f32[24,8,128]{2,1,0:T(8,128)} %get-tuple-element.23.right) | copy-start | bytes 294916
